TPU v7x, 512 devices: a whole 4x4x16 slice. The times are simulated.
512 devices in a mesh: slot: 16 (over z), seq: 8 (over y_lo, x), head: 4 (over y_hi, core).
Axes of the slice: x: 4, y: 4 (y_hi: 2, y_lo: 2; y = y_hi * 2 + y_lo), z: 16, core: 2. Of those that a mesh axis runs over, the one named last changes fastest.
Arguments:
- hidden: bfloat16 [10240, 5120], P(('slot', 'seq'), 'head')
- final_mod: float32 [16, 2, 5120], P('slot', None, 'head'), may hold values from -3 to 3
- head_weight: float32 [5120, 64], P('head'), may hold values from -0.078125 to 0.078125
- latents: float32 [10240, 64], P(('slot', 'seq')), may hold values from -6 to 6
- fresh_noise: float32 [640, 64], P('seq'), may hold values from -6 to 6
- step_index: int32 [16], replicated, may hold values from 1 to 48, as said below
- slot_group: int32 [16], replicated, may hold values from 0 to 15, each once
- group_mask: int32 [16, 16], replicated, may hold values from 0 to 1, as said below
- patch_weight: bfloat16 [64, 5120], replicated, may hold values from -0.75 to 0.75
- block_mod: float32 [16, 2, 5120], P('slot'), may hold values from -3 to 3
- qkv_weight: bfloat16 [5120, 3, 4096], P(None, None, ('seq', 'head')), may hold values from -0.078125 to 0.078125
Outputs:
- stepped: float32 [10240, 64], P(('slot', 'seq'))
- attn_out: bfloat16 [10240, 4096], P('slot', ('seq', 'head'))
Inputs may be any that keep to these rules, and one draw needn't show every extreme that they name: `step_index`: falls strictly from slot to slot; slot s lies in (16 - s - 1) * 3 + 1 to (16 - s) * 3, slot 0 at the top. `group_mask`: row i is 1 exactly on a run of groups that ends at group i, 0 elsewhere.
All inputs are finite; a program needn't handle non-finite values.
Results may differ from a plain program's by a relative error of at most 0.0049.
Values may be sent and summed in bfloat16 or wider, within the bound.
A program may use at most 64 MiB of HBM per device.

v0:
```python
import math

import jax
import jax.numpy as jnp
from jax import lax
from jax.sharding import PartitionSpec as P

D = 5120
HD = 128
STEPS = 48


EPS_NORM = 1e-06


def shifted_2(shard, axis, by):
    length = lax.axis_size(axis)
    pairs = [(i, i + by) for i in range(length) if 0 <= i + by < length]
    return lax.ppermute(shard, axis, pairs)


def sigma_of(levels):
    ratio = levels.astype(jnp.float32) / STEPS
    return 5.0 * ratio / (1.0 + 4.0 * ratio)


def layer_norm(matrix):
    row_mean = jnp.mean(matrix, axis=-1, keepdims=True)
    centred = matrix - row_mean
    spread = jnp.mean(centred * centred, axis=-1, keepdims=True)
    return centred * lax.rsqrt(spread + EPS_NORM)


def rms_heads(block):
    shaped = block.reshape(block.shape[0], -1, HD)
    return (
        shaped * lax.rsqrt(jnp.mean(shaped * shaped, axis=-1, keepdims=True) + EPS_NORM)
    ).astype(jnp.bfloat16)


def local(
    hidden,
    final_mod,
    head_weight,
    latents,
    fresh_noise,
    step_index,
    slot_group,
    group_mask,
    patch_weight,
    block_mod,
    qkv_weight,
):
    highest = lax.Precision.HIGHEST
    slot_index = lax.axis_index("slot")
    slot_ids = jnp.arange(step_index.shape[0], dtype=jnp.int32)
    own_slot = slot_ids == slot_index
    features = hidden.astype(jnp.float32)
    out_gain = 1.0 + final_mod[0, 0]
    out_shift = final_mod[0, 1]
    row_sum, row_square = lax.psum((jnp.sum(features, 1), jnp.sum(features * features, 1)), "head")
    row_mean = row_sum[:, None] / D
    row_scale = lax.rsqrt(row_square[:, None] / D - row_mean * row_mean + EPS_NORM)
    final_normed = (features - row_mean) * row_scale * out_gain + out_shift
    velocity = lax.psum(jnp.dot(final_normed, head_weight, precision=highest), "head")
    sigma_now = sigma_of(step_index)
    sigma_next = sigma_of(jnp.concatenate([step_index[1:], jnp.zeros((1,), jnp.int32)]))
    delta = jnp.sum(jnp.where(own_slot, sigma_next - sigma_now, 0.0))
    stepped = latents + delta * velocity
    arrived = shifted_2(stepped, "slot", 1)
    shifted = jnp.where(slot_index == 0, fresh_noise, arrived)
    mod_gain = 1.0 + block_mod[0, 0]
    mod_shift = block_mod[0, 1]
    embedded = jnp.dot(
        shifted.astype(jnp.bfloat16), patch_weight, preferred_element_type=jnp.float32
    )
    projected = jnp.einsum(
        "td,dcw->tcw",
        lax.all_gather(
            (layer_norm(embedded) * mod_gain + mod_shift).astype(jnp.bfloat16),
            "seq",
            axis=0,
            tiled=True,
        ),
        qkv_weight,
        preferred_element_type=jnp.float32,
    )
    group_rows = projected.shape[0]
    queries = rms_heads(projected[:, 0])
    keys = rms_heads(projected[:, 1])
    values = projected[:, 2].reshape(group_rows, -1, HD).astype(jnp.bfloat16)
    own_group = jnp.sum(jnp.where(own_slot, slot_group, 0))
    mask_row = jnp.sum(jnp.where((slot_ids == own_group)[:, None], group_mask, 0), 0)
    visible = jnp.sum(
        jnp.where(slot_group[:, None] == slot_ids[None, :], mask_row[None, :], 0), 1
    ).astype(jnp.float32)

    def attend(running, key_block, value_block, keep_rows):
        value_total, weight_total = running
        scores = jnp.einsum(
            "thd,shd->hts", queries, key_block, preferred_element_type=jnp.float32
        ) / math.sqrt(HD)
        weights = jnp.exp(scores) * keep_rows[None, None, :]
        probs = weights.astype(jnp.bfloat16)
        value_total = value_total + jnp.einsum(
            "hts,shd->thd", probs, value_block, preferred_element_type=jnp.float32
        )
        return (value_total, weight_total + jnp.sum(weights, 2))

    head_count = queries.shape[1]
    initial = (
        jnp.zeros((group_rows, head_count, HD), jnp.float32),
        jnp.zeros((head_count, group_rows), jnp.float32),
    )
    key_part = lax.all_gather(keys, "slot", axis=0, tiled=True)
    value_part = lax.all_gather(values, "slot", axis=0, tiled=True)
    length = key_part.shape[0]

    def one_block(block_index, current):
        block_start = block_index * group_rows
        key_block = lax.dynamic_slice_in_dim(key_part, block_start, group_rows, 0)
        value_block = lax.dynamic_slice_in_dim(value_part, block_start, group_rows, 0)
        owners = (block_start + jnp.arange(group_rows, dtype=jnp.int32)) // group_rows
        keep_rows = jnp.sum(
            jnp.where(owners[:, None] == slot_ids[None, :], visible[None, :], 0.0), 1
        )
        return attend(current, key_block, value_block, keep_rows)

    value_total, weight_total = lax.fori_loop(0, length // group_rows, one_block, initial)
    attended = value_total / jnp.transpose(weight_total)[:, :, None]
    return (stepped, attended.astype(jnp.bfloat16).reshape(group_rows, head_count * HD))


def solution(mesh):
    in_specs = (
        P(("slot", "seq"), "head"),
        P("slot", None, "head"),
        P("head", None),
        P(("slot", "seq"), None),
        P("seq", None),
        P(),
        P(),
        P(),
        P(),
        P("slot", None, None),
        P(None, None, ("seq", "head")),
    )
    out_specs = (P(("slot", "seq"), None), P("slot", ("seq", "head")))
    return jax.shard_map(local, mesh=mesh, in_specs=in_specs, out_specs=out_specs, check_vma=False)
```

profile of v0, /device:TPU:2, one launch (start us, length us, event | category | flops | bytes accessed | tf_op | source)
XLA Modules:
  0.0 342.2 jit_solution(12182570052322787760)
XLA Ops:
  9.2 10.1 %all-reduce = (f32[80]{0:T(128)S(1)}, f32[80]{0:T(128)S(1)}) all-reduce(f32[80]{0:T(128)S(1)} %get-tuple-element.254, f32[80]{0:T(128)S(1)} %get-tuple-element.253), channel_id=1, replica_groups=mesh['slot'=16,'seq'=8,'head'=4] {'head'}, use_global_device_ids=true, to_apply=%region_4.0 | all-reduce | flops 160 | bytes 1280 | tf_op jit(solution)/shard_map/psum | solution.py:61
  19.3 1.7 fusion.16
  21.0 13.3 %psum.23 = f32[80,64]{0,1:T(8,128)S(1)} all-reduce(f32[80,64]{0,1:T(8,128)S(1)} %fusion.16), channel_id=1, replica_groups=mesh['slot'=16,'seq'=8,'head'=4] {'head'}, use_global_device_ids=true, to_apply=%region_5.6 | all-reduce | flops 5120 | bytes 40960 | tf_op jit(solution)/shard_map/psum | solution.py:65
  36.4 2.0 fusion.28
  38.4 3.8 %collective-permute-start = (bf16[80,64]{0,1:T(8,128)(2,1)S(1)}, bf16[80,64]{0,1:T(8,128)(2,1)S(1)}, u32[]{:S(2)}, u32[]{:S(2)}) collective-permute-start(bf16[80,64]{0,1:T(8,128)(2,1)S(1)} %get-tuple-element.273), channel_id=1, source_target_pairs={{0,32},{32,64},{64,96},{96,128},{128,160},{160,192},{192,224},{224... | collective-permute-start | bytes 30728 | tf_op jit(solution)/shard_map/ppermute | solution.py:19
  46.6 6.3 %copy.23 = bf16[5120,3,128]{0,2,1:T(8,128)(2,1)} copy(bf16[5120,3,128]{2,0,1:T(8,128)(2,1)} %param.23) | data formatting | bytes 7864320 | tf_op args[10]
  52.9 77.1 %all-gather.4.cloned.1.call-done = bf16[640,5120]{1,0:T(8,128)(2,1)} async-done(((bf16[80,5120]{1,0:T(8,128)(2,1)}), bf16[640,5120]{1,0:T(8,128)(2,1)}) %all-gather.4.cloned.1.call-update) | async-done | bytes 6553616 | tf_op jit(solution)/shard_map/all_gather | solution.py:79
  130.0 7.2 %fusion.31 = f32[640,384]{0,1:S(1)} fusion(bf16[640,5120]{1,0:T(8,128)(2,1)} %all-gather.4.cloned.1.call-done, bf16[5120,384]{0,1:T(8,128)(2,1)} %bitcast.42), kind=kOutput, calls=%fused_computation.67 | convolution fusion | flops 2516582400 | bytes 11468800
  140.7 73.9 %all-gather.8.cloned.1.call-done = bf16[10240,1,128]{0,2,1:T(8,128)(2,1)} async-done(((bf16[640,1,128]{0,2,1:T(8,128)(2,1)}), bf16[10240,1,128]{0,2,1:T(8,128)(2,1)}) %all-gather.8.cloned.1.call-update) | async-done | bytes 2621456 | tf_op jit(solution)/shard_map/all_gather | solution.py:115
  214.6 74.1 %all-gather.6.cloned.1.call-done = bf16[10240,1,128]{0,2,1:T(8,128)(2,1)} async-done(((bf16[640,1,128]{0,2,1:T(8,128)(2,1)}), bf16[10240,1,128]{0,2,1:T(8,128)(2,1)}) %all-gather.6.cloned.1.call-update) | async-done | bytes 2621456 | tf_op jit(solution)/shard_map/all_gather | solution.py:116
  288.8 45.8 %while.18 = (s32[]{:T(128)}, f32[640,1,128]{0,2,1:T(8,128)S(1)}, f32[1,640]{1,0:T(1,128)S(1)}, bf16[10240,1,128]{0,2,1:T(8,128)(2,1)}, bf16[10240,1,128]{0,2,1:T...) while((s32[]{:T(128)}, f32[640,1,128]{0,2,1:T(8,128)S(1)}, ...), condition=%wide.region_16.17_spmd.clone, body=%wide.region_13.16_spmd.clone.sunk | while | flops 211553920 | bytes 2806002 | solution.py:129
  288.9 1.5 fusion.44
  297.5 1.5 fusion.44
  300.3 1.5 fusion.44
  303.2 1.5 fusion.44
  306.1 1.5 fusion.44
  308.9 1.5 fusion.44
  311.8 1.5 fusion.44
  314.7 1.5 fusion.44
  317.5 1.5 fusion.44
  320.4 1.5 fusion.44
  323.3 1.5 fusion.44
  326.1 1.5 fusion.44
  329.0 1.5 fusion.44
  (106 shorter events, 38.9 us)
Async XLA Ops:
  7.2 36.5 %copy-start = (bf16[64,5120]{1,0:T(8,128)(2,1)S(1)}, bf16[64,5120]{1,0:T(8,128)(2,1)}, u32[]{:S(2)}) copy-start(bf16[64,5120]{1,0:T(8,128)(2,1)} %param.21) | copy-start | bytes 1966084
  7.2 122.8 %all-gather.4.cloned.1.call-start = ((), (), s32[]{:S(2)}) async-start(), calls=%async_computation | async-start | bytes 7372800 | tf_op jit(solution)/shard_map/all_gather | solution.py:79
  38.4 5.2 %collective-permute-start = (bf16[80,64]{0,1:T(8,128)(2,1)S(1)}, bf16[80,64]{0,1:T(8,128)(2,1)S(1)}, u32[]{:S(2)}, u32[]{:S(2)}) collective-permute-start(bf16[80,64]{0,1:T(8,128)(2,1)S(1)} %get-tuple-element.273), channel_id=1, source_target_pairs={{0,32},{32,64},{64,96},{96,128},{128,160},{160,192},{192,224},{224... | collective-permute-start | bytes 30728 | tf_op jit(solution)/shard_map/ppermute | solution.py:19
  46.5 168.1 %all-gather.8.cloned.1.call-start = ((), (), s32[]{:S(2)}) async-start(), calls=%async_computation.2 | async-start | bytes 2785280 | tf_op jit(solution)/shard_map/all_gather | solution.py:115
  137.2 1.6 copy-start.2
  137.2 3.0 copy-start.1
  138.1 150.7 %all-gather.6.cloned.1.call-start = ((), (), s32[]{:S(2)}) async-start(), calls=%async_computation.1 | async-start | bytes 2785280 | tf_op jit(solution)/shard_map/all_gather | solution.py:116
Sparse Core Ops, SparseCore 0:
  46.6 83.3 all-gather.3
  138.2 76.3 all-gather.7
  217.3 71.4 all-gather.5
where the time goes:
time: 343 us; the launch traced here: 342 us
  waiting for transfers between devices  226 us (66%)
  matrix products  53.4 us (16%)
  blocking collectives  23.4 us (7%)
  between operations  13.9 us (4%)
  other arithmetic  12.8 us (4%)
  local copies, waits for them, and re-layouts  8.08 us (2%)
  starting transfers between devices  3.93 us (1%)
    all_gather x1, waiting for transfers between devices, local(): lax.all_gather((layer_norm(embedded) * mod_gain + mod_shift).astype(jnp.b...  77.1 us
    all_gather x1, waiting for transfers between devices, local(): value_part = lax.all_gather(values, 'slot', axis=0, tiled=True)  74.1 us
    all_gather x1, waiting for transfers between devices, local(): key_part = lax.all_gather(keys, 'slot', axis=0, tiled=True)  73.9 us
    dot_general x16, matrix products, attend(): jnp.einsum('thd,shd->hts', queries, key_block, preferred_element_type=jnp...  23.2 us
    dot_general x16, matrix products, attend(): jnp.einsum('hts,shd->thd', probs, value_block, preferred_element_type=jnp...  20 us
    psum x1, blocking collectives, local(): lax.psum(jnp.dot(final_normed, head_weight, precision=highest), 'head')  13.3 us
    psum x1, blocking collectives, local(): lax.psum((jnp.sum(features, 1), jnp.sum(features * features, 1)), 'head')  10.1 us
    unnamed x1, matrix products  7.23 us
  transfers between devices with their start and end apart: 4, of which 4 were waited for; matrix products, arithmetic and copies ran while one was open for 3% of the time, Pallas kernels for 0%

commit v1 on v0

v1 whole, which is shorter than its diff:
```python
import functools
import math

import jax
import jax.numpy as jnp
from jax import lax
from jax.experimental import pallas as pl
from jax.experimental.pallas import tpu as pltpu
from jax.sharding import PartitionSpec as P

D = 5120
HD = 128
STEPS = 48
PATCH = 64
SLOTS = 16
SEQ = 8
HEADS = 4
TOK = 80
HALF = 40
XROWS = 48
MROWS = 16
FEAT = D // SEQ
EPS = 1e-06
MESH = pl.DeviceIdType.MESH
HIGHEST = lax.Precision.HIGHEST
F32 = jnp.float32
BF16 = jnp.bfloat16
NT = (((1,), (1,)), ((), ()))
NEAR_EVEN = (0, 2, 14, 4, 12, 6, 10, 8)
NEAR_ODD = (1, 15, 3, 13, 5, 11, 7, 9)


def remote(src, dst, send_sem, recv_sem, device_id):
    return pltpu.make_async_remote_copy(
        src_ref=src,
        dst_ref=dst,
        send_sem=send_sem,
        recv_sem=recv_sem,
        device_id=device_id,
        device_id_type=MESH,
    )


class Spread:
    def __init__(self, buf, zs, zr, qs, qr, cs, cr):
        self.buf = buf
        self.zs, self.zr, self.qs, self.qr, self.cs, self.cr = zs, zr, qs, qr, cs, cr
        self.slot = lax.axis_index("slot")
        self.seq = lax.axis_index("seq")
        self.head = lax.axis_index("head")
        self.core = lax.rem(self.head, 2)
        self.own = lax.rem(self.slot, 2) == self.core
        self.other_core = self.head + 1 - 2 * self.core

    def source(self, i, mine=True):
        near = jnp.where(self.own, NEAR_EVEN[i], NEAR_ODD[i]) if mine else jnp.where(
            self.own, NEAR_ODD[i], NEAR_EVEN[i]
        )
        return lax.rem(self.slot + near, SLOTS)

    def slot_copy(self, k):
        block = self.buf.at[self.slot, self.seq]
        return remote(
            block, block, self.zs.at[k], self.zr.at[self.slot], {"slot": lax.rem(self.slot + k, SLOTS)}
        )

    def slot_send(self):
        @pl.when(self.own)
        def _():
            @pl.loop(1, SLOTS)
            def _(k):
                self.slot_copy(k).start()

    def slot_wait(self, i):
        src = self.source(i)
        block = self.buf.at[src, self.seq]

        def wait():
            remote(block, block, self.zs.at[0], self.zr.at[src], {"slot": self.slot}).wait_recv()

        if i == 0:
            pl.when(jnp.logical_not(self.own))(wait)
        else:
            wait()

    def seq_send(self, i):
        src = self.source(i)
        block = self.buf.at[src, self.seq]

        @pl.loop(1, SEQ)
        def _(k):
            remote(
                block, block, self.qs.at[src], self.qr.at[src], {"seq": lax.rem(self.seq + k, SEQ)}
            ).start()

    def seq_all(self, src):
        blocks = self.buf.at[src, pl.ds(0, SEQ - 1)]
        return remote(blocks, blocks, self.qs.at[src], self.qr.at[src], {"seq": self.seq})

    def core_copy(self, src):
        blocks = self.buf.at[src]
        return remote(
            blocks, blocks, self.cs.at[src], self.cr.at[src], {"head": self.other_core}
        )

    def core_send(self, i):
        src = self.source(i)
        self.seq_all(src).wait_recv()
        self.core_copy(src).start()

    def core_wait(self, i):
        self.core_copy(self.source(i, mine=False)).wait_recv()

    def finish(self):
        @pl.when(self.own)
        def _():
            @pl.loop(1, SLOTS)
            def _(k):
                self.slot_copy(k).wait_send()

        for i in range(SLOTS // 2):
            src = self.source(i)
            self.seq_all(src).wait_send()
            self.core_copy(src).wait_send()


def partial_velocity(hidden, final_mod, head_t, msg):
    h = hidden[...].astype(F32)
    mean = jnp.mean(h, axis=1, keepdims=True)
    centred = h - mean
    spread = jnp.sum(centred * centred, axis=1, keepdims=True)
    weight = head_t[...] * (1.0 + final_mod[0, 0:1, :])
    part = lax.dot_general(centred, weight, NT, precision=HIGHEST, preferred_element_type=F32)
    ones = jnp.ones((8, weight.shape[1]), F32)
    gain_sum = lax.dot_general(ones, weight, NT, precision=HIGHEST, preferred_element_type=F32)
    shift = jnp.broadcast_to(final_mod[0, 1:2, :], ones.shape)
    shift_sum = lax.dot_general(shift, head_t[...], NT, precision=HIGHEST, preferred_element_type=F32)
    lane = lax.broadcasted_iota(jnp.int32, (TOK, PATCH), 1)
    stats = jnp.where(lane == 0, mean, jnp.where(lane == 1, spread, 0.0))
    msg[0:TOK, :] = jnp.concatenate([part, stats], axis=1)
    msg[TOK : TOK + 8, :] = jnp.concatenate([gain_sum, shift_sum], axis=1)


def whole_velocity(parts, count):
    means = [p[0:TOK, PATCH : PATCH + 1] for p in parts]
    mean = sum(means) / len(parts)
    spread = 0.0
    total = 0.0
    shift = 0.0
    for p, m in zip(parts, means):
        off = m - mean
        spread = spread + p[0:TOK, PATCH + 1 : PATCH + 2] + count * off * off
        total = total + p[0:TOK, 0:PATCH] + off * p[TOK : TOK + 1, 0:PATCH]
        shift = shift + p[TOK : TOK + 1, PATCH : 2 * PATCH]
    return total * lax.rsqrt(spread / (count * len(parts)) + EPS) + shift


def sigma_of(level):
    ratio = jnp.full((1, PATCH), level, jnp.int32).astype(F32) / STEPS
    return 5.0 * ratio / (1.0 + 4.0 * ratio)


def move_kernel(
    hidden,
    final_mod,
    head_t,
    latents_t,
    noise_t,
    step_index,
    patch_weight,
    block_mod,
    stepped_t,
    xall,
    mall,
    msg,
    got,
    ps,
    pr,
    *sems,
):
    x = Spread(xall, *sems[:6])
    m = Spread(mall, *sems[6:])
    slot, seq, head = x.slot, x.seq, x.head
    barrier = pltpu.get_barrier_semaphore()
    for axis, index, size in (("head", head, HEADS), ("seq", seq, SEQ), ("slot", slot, SLOTS)):
        for k in range(1, size):
            pl.semaphore_signal(
                barrier, inc=1, device_id={axis: lax.rem(index + k, size)}, device_id_type=MESH
            )
    partial_velocity(hidden, final_mod, head_t, msg)

    @pl.when(x.own)
    def _():
        start = pl.multiple_of(seq * FEAT, 128)
        both = block_mod[0, :, pl.ds(start, FEAT)]
        gain = 1.0 + both[0:1]
        rows = [gain[:, 128 * r : 128 * r + 128] for r in range(FEAT // 128)]
        rows += [jnp.zeros((3, 128), F32)]
        rows += [both[1:2, 128 * r : 128 * r + 128] for r in range(FEAT // 128)]
        rows += [jnp.zeros((3, 128), F32)]
        mall[slot, seq] = jnp.concatenate(rows, axis=0).astype(BF16)

    pl.semaphore_wait(barrier, HEADS + SEQ + SLOTS - 3)
    sends = [
        remote(msg, got.at[k - 1], ps.at[k - 1], pr.at[k - 1], {"head": lax.rem(head + k, HEADS)})
        for k in range(1, HEADS)
    ]
    for copy in sends:
        copy.start()
    m.slot_send()

    weight = patch_weight[...]
    gram = lax.dot_general(weight, weight, NT, preferred_element_type=F32) / D
    ones = jnp.ones((16, D), BF16)
    mean_row = lax.dot_general(ones, weight, NT, preferred_element_type=F32)[0:8] / D
    mean_outer = lax.dot_general(
        mean_row, mean_row, (((0,), (0,)), ((), ())), precision=HIGHEST, preferred_element_type=F32
    ) / 8.0
    gram = gram - mean_outer
    latents = jnp.transpose(latents_t[...])
    noise = jnp.transpose(noise_t[...])
    now = step_index[slot]
    later = jnp.where(slot == SLOTS - 1, 0, step_index[jnp.minimum(slot + 1, SLOTS - 1)])
    delta = sigma_of(later) - sigma_of(now)

    for copy in sends:
        copy.wait_recv()
    velocity = whole_velocity([msg[...]] + [got[k] for k in range(HEADS - 1)], D // HEADS)
    stepped = latents + delta * velocity
    shifted = jnp.where(slot == SLOTS - 1, noise, stepped).astype(BF16).astype(F32)
    projected = jnp.dot(shifted, gram, precision=HIGHEST, preferred_element_type=F32)
    spread = jnp.sum(projected * shifted, axis=1, keepdims=True)
    scaled = shifted * lax.rsqrt(jnp.maximum(spread, 0.0) + EPS)
    block = jnp.concatenate([scaled[0:HALF], scaled[HALF:TOK]], axis=1)
    block = jnp.concatenate([block, jnp.zeros((XROWS - HALF, 128), F32)], axis=0).astype(BF16)

    @pl.when(x.own)
    def _():
        xall[slot, seq] = block

    x.slot_send()
    stepped_t[...] = jnp.transpose(stepped)
    count = SLOTS // 2
    for i in range(count):
        m.slot_wait(i)
        m.seq_send(i)
    for i in range(count):
        x.slot_wait(i)
        x.seq_send(i)
        m.core_send(i)
    for i in range(count):
        x.core_send(i)
    for i in range(count):
        m.core_wait(i)
        x.core_wait(i)
    for copy in sends:
        copy.wait_send()
    m.finish()
    x.finish()


def attend_kernel(
    slot_group, group_mask, xall, mall, qkv, patch_weight, out, centred, lhs, a_kv, a_q, q_ref, total
):
    slot = lax.axis_index("slot")
    weight = patch_weight[...].astype(F32)
    centred[...] = weight - jnp.mean(weight, axis=1, keepdims=True)
    base = SLOTS * PATCH

    a_kv[...] = jnp.zeros_like(a_kv)
    a_q[...] = jnp.zeros_like(a_q)
    parts = FEAT // 128

    @pl.loop(0, SEQ)
    def _(p):
        start = pl.multiple_of(p * FEAT, 128)

        @pl.loop(0, SLOTS)
        def _(b):
            mods = mall[b, p].astype(F32)
            rows = pl.ds(pl.multiple_of(b * PATCH, PATCH), PATCH)
            for r in range(parts):
                piece = centred[:, pl.ds(pl.multiple_of(start + 128 * r, 128), 128)]
                lhs[rows, 128 * r : 128 * r + 128] = (piece * mods[r : r + 1]).astype(BF16)

        for r in range(parts):
            shifts = [mall[b, p].astype(F32)[8 + r : 9 + r] for b in range(SLOTS)]
            lhs[base : base + SLOTS, 128 * r : 128 * r + 128] = jnp.concatenate(shifts, axis=0).astype(BF16)
        depth = pl.ds(start, FEAT)
        a_kv[:, 0:HD] += jnp.dot(lhs[...], qkv[1, depth, :], preferred_element_type=F32)
        a_kv[:, HD : 2 * HD] += jnp.dot(lhs[...], qkv[2, depth, :], preferred_element_type=F32)
        own = lhs[pl.ds(pl.multiple_of(slot * PATCH, PATCH), PATCH), :]
        own = jnp.concatenate([own, lhs[base : base + SLOTS, :]], axis=0)
        a_q[...] += jnp.dot(own, qkv[0, depth, :], preferred_element_type=F32)

    def tokens(src, matrix, bias):
        blocks = xall[src].reshape(SEQ * XROWS, 128)
        zero = jnp.zeros_like(matrix)
        found = []
        for pair in ([matrix, zero], [zero, matrix]):
            wide = jnp.dot(blocks, jnp.concatenate(pair, axis=0), preferred_element_type=F32)
            wide = wide.reshape(SEQ, XROWS, wide.shape[1])[:, 0:HALF]
            found.append(wide.reshape(SEQ * HALF, wide.shape[2]) + bias)
        return found

    def unit(block):
        return block * lax.rsqrt(jnp.mean(block * block, axis=1, keepdims=True) + EPS)

    first, second = tokens(
        lax.rem(slot + SLOTS - 1, SLOTS), a_q[0:PATCH].astype(BF16), a_q[pl.ds(PATCH + slot, 1), :]
    )
    scale = 1.0 / (math.sqrt(HD) * math.log(2.0))
    group = SEQ * HALF
    for at, block in ((0, first), (1, second)):
        q_ref[at * group : at * group + group, :] = (unit(block) * scale).astype(BF16)
    total[...] = jnp.zeros_like(total)
    mine = slot_group[slot]

    @pl.loop(0, SLOTS)
    def _(b):
        @pl.when(group_mask[mine, slot_group[b]] != 0)
        def _():
            rows = pl.ds(pl.multiple_of(b * PATCH, PATCH), PATCH)
            pair = tokens(
                lax.rem(b + SLOTS - 1, SLOTS), a_kv[rows, :].astype(BF16), a_kv[pl.ds(base + b, 1), :]
            )
            keys = jnp.concatenate([unit(t[:, 0:HD]) for t in pair], axis=0).astype(BF16)
            values = jnp.concatenate([t[:, HD : 2 * HD] for t in pair], axis=0).astype(BF16)
            values = jnp.concatenate([values, jnp.ones_like(values)], axis=1)
            for at in range(5):
                part = slice(at * 128, at * 128 + 128)
                scores = lax.dot_general(q_ref[part, :], keys, NT, preferred_element_type=F32)
                probs = jnp.exp2(scores).astype(BF16)
                total[part, :] += jnp.dot(probs, values, preferred_element_type=F32)

    for p in range(SEQ):
        found = []
        for half in range(2):
            rows = slice(half * group + p * HALF, half * group + p * HALF + HALF)
            found.append(total[rows, 0:HD] / total[rows, HD : 2 * HD])
        out[p * TOK : p * TOK + TOK, :] = jnp.concatenate(found, axis=0).astype(out.dtype)


def spread_sems():
    dma = pltpu.SemaphoreType.DMA
    return [dma((SLOTS,)) for _ in range(6)]


def local(
    hidden,
    final_mod,
    head_weight,
    latents,
    fresh_noise,
    step_index,
    slot_group,
    group_mask,
    patch_weight,
    block_mod,
    qkv_weight,
):
    vmem = pl.BlockSpec(memory_space=pltpu.VMEM)
    smem = pl.BlockSpec(memory_space=pltpu.SMEM)
    dma = pltpu.SemaphoreType.DMA
    stepped_t, xall, mall = pl.pallas_call(
        move_kernel,
        out_shape=(
            jax.ShapeDtypeStruct((PATCH, TOK), F32),
            jax.ShapeDtypeStruct((SLOTS, SEQ, XROWS, 128), BF16),
            jax.ShapeDtypeStruct((SLOTS, SEQ, MROWS, 128), BF16),
        ),
        in_specs=[vmem] * 5 + [smem] + [vmem] * 2,
        out_specs=(vmem,) * 3,
        scratch_shapes=[
            pltpu.VMEM((TOK + 8, 128), F32),
            pltpu.VMEM((HEADS - 1, TOK + 8, 128), F32),
            dma((HEADS - 1,)),
            dma((HEADS - 1,)),
        ]
        + spread_sems()
        + spread_sems(),
        compiler_params=pltpu.CompilerParams(
            collective_id=0, has_side_effects=True, vmem_limit_bytes=32 * 2**20
        ),
        name="move",
    )(
        hidden,
        final_mod,
        head_weight.T,
        latents.T,
        fresh_noise.T,
        step_index,
        patch_weight,
        block_mod,
    )
    rows = SLOTS * PATCH + SLOTS
    attn = pl.pallas_call(
        attend_kernel,
        out_shape=jax.ShapeDtypeStruct((SEQ * TOK, HD), BF16),
        in_specs=[smem] * 2 + [vmem] * 4,
        out_specs=vmem,
        scratch_shapes=[
            pltpu.VMEM((PATCH, D), F32),
            pltpu.VMEM((rows, FEAT), BF16),
            pltpu.VMEM((rows, 2 * HD), F32),
            pltpu.VMEM((PATCH + SLOTS, HD), F32),
            pltpu.VMEM((SEQ * TOK, HD), BF16),
            pltpu.VMEM((SEQ * TOK, 2 * HD), F32),
        ],
        compiler_params=pltpu.CompilerParams(vmem_limit_bytes=48 * 2**20),
        name="attend",
    )(slot_group, group_mask, xall, mall, jnp.transpose(qkv_weight, (1, 0, 2)), patch_weight)
    return stepped_t.T, attn


def solution(mesh):
    in_specs = (
        P(("slot", "seq"), "head"),
        P("slot", None, "head"),
        P("head", None),
        P(("slot", "seq"), None),
        P("seq", None),
        P(),
        P(),
        P(),
        P(),
        P("slot", None, None),
        P(None, None, ("seq", "head")),
    )
    out_specs = (P(("slot", "seq"), None), P("slot", ("seq", "head")))
    return jax.shard_map(local, mesh=mesh, in_specs=in_specs, out_specs=out_specs, check_vma=False)
```

time: 343 us -> 77.6 us (0.23)
  the two profiles are of different devices: /device:TPU:2 before, /device:TPU:1 now
where the time goes in v1:
time: 77.6 us; the launch traced here: 76.5 us
  Pallas kernels  66.1 us (85%)
  local copies, waits for them, and re-layouts  9.68 us (12%)
    pallas_call x1, Pallas kernels, local(): pl.pallas_call(move_kernel, out_shape=(jax.ShapeDtypeStruct((PATCH, TOK),...  42.8 us
    pallas_call x1, Pallas kernels, local(): pl.pallas_call(attend_kernel, out_shape=jax.ShapeDtypeStruct((SEQ * TOK,...  23.3 us
    unnamed x23, local copies, waits for them, and re-layouts  9.68 us

profile of v1, /device:TPU:1, one launch (start us, length us, event | category | flops | bytes accessed | tf_op | source)
XLA Modules:
  0.0 76.5 jit_solution(17686627975266515465)
XLA Ops:
  0.6 0.0 copy-start
  0.6 1.1 %copy-done = bf16[64,5120]{1,0:T(8,128)(2,1)S(1)} copy-done((bf16[64,5120]{1,0:T(8,128)(2,1)S(1)}, bf16[64,5120]{1,0:T(8,128)(2,1)}, u32[]{:S(2)}) %copy-start) | copy-done | bytes 655384
  1.7 0.0 copy-start.2
  1.7 1.0 %copy-done.2 = f32[1280,64]{0,1:T(8,128)S(1)} copy-done((f32[1280,64]{0,1:T(8,128)S(1)}, f32[1280,64]{0,1:T(8,128)}, u32[]{:S(2)}) %copy-start.2) | copy-done | bytes 327704
  2.7 0.0 copy-start.3
  2.7 0.9 %copy-done.3 = bf16[80,1280]{1,0:T(8,128)(2,1)S(1)} copy-done((bf16[80,1280]{1,0:T(8,128)(2,1)S(1)}, bf16[80,1280]{1,0:T(8,128)(2,1)}, u32[]{:S(2)}) %copy-start.3) | copy-done | bytes 204824
  3.6 0.0 copy-start.4
  3.6 0.8 %copy-done.4 = f32[1,2,5120]{2,1,0:T(2,128)S(1)} copy-done((f32[1,2,5120]{2,1,0:T(2,128)S(1)}, f32[1,2,5120]{2,1,0:T(2,128)}, u32[]{:S(2)}) %copy-start.4) | copy-done | bytes 40984
  4.4 0.0 copy-start.5
  4.4 0.8 copy-done.5
  5.2 0.0 copy-start.6
  5.2 0.8 copy-done.6
  5.9 0.0 copy-start.7
  5.9 0.7 copy-done.7
  6.6 0.7 copy-done.9
  7.3 42.8 %move.1 = (f32[64,80]{1,0:T(8,128)S(1)}, bf16[16,8,48,128]{3,2,1,0:T(8,128)(2,1)S(1)}, bf16[16,8,16,128]{3,2,1,0:T(8,128)(2,1)S(1)}) custom-call(bf16[80,1280]{1,0:T(8,128)(2,1)S(1)} %copy-done.3, f32[1,2,1280]{2,1,0:T(2,128)S(1)} %copy-done.7, f32[64,1280]{1,0:T(8,128)S(1)} %bitcast.5, f32[64,80]{1,0:T(8,128)S(1)} %bitcast.6, f32[64,80]{1,0:T(8,128)S(1)} %bitcast.7, ...), custom_call_target="tpu_custom_call" | custom-call | tf_op jit(solution)/shard_map/move/pallas_call | solution.py:365
  50.1 0.0 copy-start.1
  50.1 1.1 %copy-done.1 = bf16[64,5120]{1,0:T(8,128)(2,1)S(1)} copy-done((bf16[64,5120]{1,0:T(8,128)(2,1)S(1)}, bf16[64,5120]{1,0:T(8,128)(2,1)}, u32[]{:S(2)}) %copy-start.1) | copy-done | bytes 655384
  51.2 0.0 copy-start.8
  51.2 0.7 copy-done.8
  51.9 0.0 copy-start.10
  51.9 0.7 copy-done.10
  52.6 23.3 %attend.1 = bf16[640,128]{1,0:T(8,128)(2,1)} custom-call(s32[16]{0:T(128)S(1)} %copy-done.10, s32[16,16]{1,0:T(8,128)S(1)} %copy-done.8, bf16[16,8,48,128]{3,2,1,0:T(8,128)(2,1)S(1)} %get-tuple-element.6.xall, bf16[16,8,16,128]{3,2,1,0:T(8,128)(2,1)S(1)} %get-tuple-element.7.mall, bf16[3,5120,128]{2,1,0:T(8,128)(2,1)} %bitcast.9, bf16[64,5120]{1,0:T(8,128)(2,1)S(1)} %copy-done.1), custom_call_target="tpu_custom_call" | custom-call | tf_op jit(solution)/shard_map/attend/pallas_call | solution.py:397
  75.8 0.6 copy.14
  (1 shorter events, 0.0 us)
Async XLA Ops:
  0.6 1.1 %copy-start = (bf16[64,5120]{1,0:T(8,128)(2,1)S(1)}, bf16[64,5120]{1,0:T(8,128)(2,1)}, u32[]{:S(2)}) copy-start(bf16[64,5120]{1,0:T(8,128)(2,1)} %patch_weight.3) | copy-start | bytes 1966084
  1.7 1.0 %copy-start.2 = (f32[1280,64]{0,1:T(8,128)S(1)}, f32[1280,64]{0,1:T(8,128)}, u32[]{:S(2)}) copy-start(f32[1280,64]{0,1:T(8,128)} %param.13) | copy-start | bytes 983044
  2.7 0.9 %copy-start.3 = (bf16[80,1280]{1,0:T(8,128)(2,1)S(1)}, bf16[80,1280]{1,0:T(8,128)(2,1)}, u32[]{:S(2)}) copy-start(bf16[80,1280]{1,0:T(8,128)(2,1)} %hidden.1) | copy-start | bytes 614404
  3.6 0.8 %copy-start.4 = (f32[1,2,5120]{2,1,0:T(2,128)S(1)}, f32[1,2,5120]{2,1,0:T(2,128)}, u32[]{:S(2)}) copy-start(f32[1,2,5120]{2,1,0:T(2,128)} %block_mod.1) | copy-start | bytes 122884
  4.4 0.8 copy-start.5
  5.2 0.8 copy-start.6
  5.9 0.7 copy-start.7
  6.6 0.7 copy-start.9
  50.1 1.1 %copy-start.1 = (bf16[64,5120]{1,0:T(8,128)(2,1)S(1)}, bf16[64,5120]{1,0:T(8,128)(2,1)}, u32[]{:S(2)}) copy-start(bf16[64,5120]{1,0:T(8,128)(2,1)} %patch_weight.3) | copy-start | bytes 1966084
  51.2 0.7 copy-start.8
  51.9 0.7 copy-start.10

commit v2 on v1

v2 whole, which is shorter than its diff:
```python
import math

import jax
import jax.numpy as jnp
from jax import lax
from jax.experimental import pallas as pl
from jax.experimental.pallas import tpu as pltpu
from jax.sharding import PartitionSpec as P

D = 5120
HD = 128
STEPS = 48
PATCH = 64
SLOTS = 16
SEQ = 8
HEADS = 4
CHUNKS = D // 128
TOK = 80
HALF = 40
XROWS = 48
MROWS = 16
FEAT = D // SEQ
EPS = 1e-06
MESH = pl.DeviceIdType.MESH
HIGHEST = lax.Precision.HIGHEST
F32 = jnp.float32
BF16 = jnp.bfloat16
NT = (((1,), (1,)), ((), ()))
PAIRS = SLOTS // 2
ROW = SEQ // 2
PARTS = FEAT // 128
KEYS = 2 * SEQ * TOK


def remote(src, dst, send_sem, recv_sem, device_id):
    return pltpu.make_async_remote_copy(
        src_ref=src,
        dst_ref=dst,
        send_sem=send_sem,
        recv_sem=recv_sem,
        device_id=device_id,
        device_id_type=MESH,
    )


class Spread:
    def __init__(self, buf, shift, sems):
        self.buf = buf
        self.zs, self.zr, self.qs, self.qr, self.ys, self.yr, self.cs, self.cr = sems
        self.shift = shift
        self.slot = lax.axis_index("slot")
        self.seq = lax.axis_index("seq")
        self.head = lax.axis_index("head")
        self.core = lax.rem(self.head, 2)
        self.own = lax.rem(self.slot, 2) == self.core
        self.other_core = self.head + 1 - 2 * self.core
        self.low = self.seq // ROW
        self.at = lax.rem(self.seq, ROW)

    def source(self, i, mine=True):
        odd = lax.rem(i, 2) == 1
        even_list = jnp.where(odd, i + 1, SLOTS - i)
        odd_list = jnp.where(odd, SLOTS - i, i + 1)
        if self.shift:
            even_list, odd_list = odd_list + 1, even_list + 1
        near = jnp.where(self.own, even_list, odd_list) if mine else jnp.where(self.own, odd_list, even_list)
        return lax.rem(self.slot + near, SLOTS)

    def half(self, src, low):
        return self.buf.at[src, pl.ds(low * ROW, ROW)]

    def slot_copy(self, k):
        block = self.buf.at[self.slot, self.seq]
        return remote(
            block, block, self.zs.at[k], self.zr.at[self.slot], {"slot": lax.rem(self.slot + k, SLOTS)}
        )

    def slot_send(self):
        @pl.when(self.own)
        def _():
            @pl.loop(1, SLOTS)
            def _(k):
                self.slot_copy(k).start()

    def slot_wait(self, i):
        src = self.source(i)
        block = self.buf.at[src, self.seq]

        @pl.when(src != self.slot)
        def _():
            remote(block, block, self.zs.at[0], self.zr.at[src], {"slot": self.slot}).wait_recv()

    def row_send(self, i):
        src = self.source(i)
        block = self.buf.at[src, self.seq]
        for k in range(1, ROW):
            to = self.low * ROW + lax.rem(self.at + k, ROW)
            remote(block, block, self.qs.at[src], self.qr.at[src], {"seq": to}).start()

    def row_all(self, src):
        blocks = self.buf.at[src, pl.ds(0, ROW - 1)]
        return remote(blocks, blocks, self.qs.at[src], self.qr.at[src], {"seq": self.seq})

    def side_copy(self, i):
        src = self.source(i)
        blocks = self.half(src, self.low)
        head = lax.rem(self.head + 2 * lax.rem(i, 2), HEADS)
        seq = (1 - self.low) * ROW + self.at
        return remote(blocks, blocks, self.ys.at[src], self.yr.at[src], {"seq": seq, "head": head})

    def core_copy(self, src, low):
        blocks = self.half(src, low)
        return remote(blocks, blocks, self.cs.at[src], self.cr.at[src], {"head": self.other_core})

    def core_all(self, src):
        blocks = self.buf.at[src]
        return remote(blocks, blocks, self.cs.at[src], self.cr.at[src], {"head": self.other_core})

    def first(self, i):
        self.slot_wait(i)
        self.row_send(i)

    def second(self, i):
        src = self.source(i)
        self.row_all(src).wait_recv()
        self.side_copy(i).start()
        self.core_copy(src, self.low).start()

    def third(self, i):
        src = self.source(i)
        self.side_copy(i).wait_recv()
        self.core_copy(src, 1 - self.low).start()

    def fourth(self, i):
        self.core_all(self.source(i, mine=False)).wait_recv()

    def finish(self):
        @pl.when(self.own)
        def _():
            @pl.loop(1, SLOTS)
            def _(k):
                self.slot_copy(k).wait_send()

        @pl.loop(0, PAIRS)
        def _(i):
            src = self.source(i)
            self.row_all(src).wait_send()
            self.side_copy(i).wait_send()
            self.core_all(src).wait_send()


def split(value, count):
    found = []
    for _ in range(count):
        part = value.astype(BF16)
        found.append(part)
        value = value - part.astype(F32)
    return found


def partial_velocity(hidden, final_mod, head_t, msg):
    h = hidden[...]
    wide = h.astype(F32)
    mean = jnp.mean(wide, axis=1, keepdims=True)
    centred = wide - mean
    spread = jnp.sum(centred * centred, axis=1, keepdims=True)
    gained = head_t[...] * (1.0 + final_mod[0, 0:1, :])
    gain_sum = jnp.sum(gained, axis=1, keepdims=True)
    shift_sum = jnp.sum(head_t[...] * final_mod[0, 1:2, :], axis=1, keepdims=True)
    stack = jnp.concatenate(split(gained, 3), axis=0)
    parts = lax.dot_general(h, stack, NT, preferred_element_type=F32)
    part = parts[:, 0:PATCH] + parts[:, PATCH : 2 * PATCH] + parts[:, 2 * PATCH : 3 * PATCH]
    lane = lax.broadcasted_iota(jnp.int32, (TOK, PATCH), 1)
    pad = jnp.zeros((TOK - PATCH, 1), F32)
    gain_sum = jnp.concatenate([gain_sum, pad], axis=0)
    shift_sum = jnp.concatenate([shift_sum, pad], axis=0)
    stats = jnp.where(lane == 0, mean, jnp.where(lane == 1, spread, 0.0))
    stats = jnp.where(lane == 2, gain_sum, jnp.where(lane == 3, shift_sum, stats))
    msg[...] = jnp.concatenate([part, stats], axis=1)


def whole_velocity(parts, count):
    total = sum(parts)
    mean = total[:, PATCH : PATCH + 1] / len(parts)
    spread = total[:, PATCH + 1 : PATCH + 2]
    for p in parts:
        off = p[:, PATCH : PATCH + 1] - mean
        spread = spread + count * off * off
    turned = jnp.transpose(jnp.concatenate([total, jnp.zeros((128 - TOK, 128), F32)], axis=0))
    gain_row = turned[PATCH + 2 : PATCH + 3, 0:PATCH]
    shift_row = turned[PATCH + 3 : PATCH + 4, 0:PATCH]
    scale = lax.rsqrt(spread / (count * len(parts)) + EPS)
    return (total[:, 0:PATCH] - mean * gain_row) * scale + shift_row


def sigma_of(level):
    ratio = jnp.full((1, PATCH), level, jnp.int32).astype(F32) / STEPS
    return 5.0 * ratio / (1.0 + 4.0 * ratio)


def unit(block):
    return block * lax.rsqrt(jnp.mean(block * block, axis=1, keepdims=True) + EPS)


def kernel(
    hidden_in,
    final_mod_in,
    head_in,
    latents_in,
    noise_in,
    step_in,
    group_in,
    mask_in,
    patch_in,
    block_in,
    qkv_in,
    stepped_out,
    attn_out,
    hidden,
    final_mod,
    head_t,
    latents_t,
    noise_t,
    step_index,
    slot_group,
    group_mask,
    patch_weight,
    block_mod,
    q_weight,
    kv_weight,
    stepped_t,
    attn,
    xall,
    mall,
    msg,
    got,
    centred,
    lhs,
    a_kv,
    b_kv,
    q_ref,
    keys,
    values,
    total,
    local_sem,
    ps,
    pr,
    *sems,
):
    x = Spread(xall, 0, sems[:8])
    m = Spread(mall, 1, sems[8:])
    slot, seq, head = x.slot, x.seq, x.head
    loads = [
        pltpu.make_async_copy(src, dst, local_sem.at[i])
        for i, (src, dst) in enumerate(
            (
                (hidden_in, hidden),
                (final_mod_in, final_mod),
                (head_in, head_t),
                (block_in, block_mod),
                (patch_in, patch_weight),
                (latents_in, latents_t),
                (noise_in, noise_t),
                (step_in, step_index),
                (group_in, slot_group),
                (mask_in, group_mask),
                (qkv_in.at[0], q_weight),
                (qkv_in.at[1], kv_weight.at[:, 0:HD]),
                (qkv_in.at[2], kv_weight.at[:, HD : 2 * HD]),
            )
        )
    ]
    for copy in loads:
        copy.start()
    barrier = pltpu.get_barrier_semaphore()

    def greet(device_id):
        pl.semaphore_signal(barrier, inc=1, device_id=device_id, device_id_type=MESH)

    for k in range(1, SLOTS):
        greet({"slot": lax.rem(slot + k, SLOTS)})
    for k in range(1, HEADS):
        greet({"head": lax.rem(head + k, HEADS)})
    for k in range(1, ROW):
        greet({"seq": x.low * ROW + lax.rem(x.at + k, ROW)})
    side = (1 - x.low) * ROW + x.at
    greet({"seq": side})
    greet({"seq": side, "head": lax.rem(head + 2, HEADS)})

    for copy in loads[:4]:
        copy.wait()
    partial_velocity(hidden, final_mod, head_t, msg)
    sub = lax.broadcasted_iota(jnp.int32, (MROWS, 128), 0)

    @pl.when(x.own)
    def _():
        start = pl.multiple_of(seq * FEAT, 128)
        gain = 1.0 + block_mod[0, 0:1, pl.ds(start, FEAT)]
        high, low = split(block_mod[0, 1:2, pl.ds(start, FEAT)], 2)
        rows = []
        for row in (gain, high.astype(F32), low.astype(F32)):
            rows += [row[:, 128 * r : 128 * r + 128] for r in range(PARTS)]
        rows += [jnp.zeros((1, 128), F32)]
        mall[slot, seq] = jnp.concatenate(rows, axis=0).astype(BF16)

    pl.semaphore_wait(barrier, SLOTS + HEADS + ROW - 3 + 2)
    sends = [
        remote(msg, got.at[k - 1], ps.at[k - 1], pr.at[k - 1], {"head": lax.rem(head + k, HEADS)})
        for k in range(1, HEADS)
    ]
    for copy in sends:
        copy.start()
    m.slot_send()

    for copy in loads[4:]:
        copy.wait()
    weight = patch_weight[...]
    gram = lax.dot_general(weight, weight, NT, preferred_element_type=F32) / D
    ones = jnp.ones((16, D), BF16)
    mean_row = lax.dot_general(ones, weight, NT, preferred_element_type=F32)[0:8] / D
    mean_outer = lax.dot_general(
        mean_row, mean_row, (((0,), (0,)), ((), ())), precision=HIGHEST, preferred_element_type=F32
    ) / 8.0
    gram = gram - mean_outer
    latents = jnp.transpose(latents_t[...])
    noise = jnp.transpose(noise_t[...])
    now = step_index[slot]
    later = jnp.where(slot == SLOTS - 1, 0, step_index[jnp.minimum(slot + 1, SLOTS - 1)])
    delta = sigma_of(later) - sigma_of(now)

    for copy in sends:
        copy.wait_recv()
    velocity = whole_velocity([msg[...]] + [got[k] for k in range(HEADS - 1)], D // HEADS)
    stepped = latents + delta * velocity
    shifted = jnp.where(slot == SLOTS - 1, noise, stepped).astype(BF16).astype(F32)
    projected = jnp.dot(shifted, gram, precision=HIGHEST, preferred_element_type=F32)
    spread = jnp.sum(projected * shifted, axis=1, keepdims=True)
    scaled = shifted * lax.rsqrt(jnp.maximum(spread, 0.0) + EPS)
    block = jnp.concatenate([scaled[0:HALF], scaled[HALF:TOK]], axis=1)
    block = jnp.concatenate([block, jnp.zeros((XROWS - HALF, 128), F32)], axis=0).astype(BF16)

    @pl.when(x.own)
    def _():
        xall[slot, seq] = block

    x.slot_send()
    stepped_t[...] = jnp.transpose(stepped)
    stepped_copy = pltpu.make_async_copy(stepped_t, stepped_out, local_sem.at[0])
    stepped_copy.start()

    wide = weight.astype(F32)
    centred[...] = wide - jnp.mean(wide, axis=1, keepdims=True)
    own_rows = PATCH + MROWS
    for c in range(CHUNKS):
        lanes = slice(128 * c, 128 * c + 128)
        gain = 1.0 + block_mod[0, 0:1, lanes]
        high, low = split(block_mod[0, 1:2, lanes], 2)
        lhs[0:PATCH, lanes] = (centred[:, lanes] * gain).astype(BF16)
        shifts = jnp.where(sub == 0, high.astype(F32), jnp.where(sub == 1, low.astype(F32), 0.0))
        lhs[PATCH:own_rows, lanes] = shifts.astype(BF16)
    found = jnp.dot(lhs[0:own_rows, :], q_weight[...], preferred_element_type=F32)
    a_q = found[0:PATCH]
    b_q = jnp.sum(found[PATCH:own_rows], axis=0, keepdims=True)

    def build(k):
        sources = [m.source(2 * k + e, mine) for e in range(2) for mine in (True, False)]

        for at, src in enumerate(sources):
            first = at * own_rows

            @pl.loop(0, SEQ)
            def _(p):
                mods = mall[src, p].astype(F32)
                for r in range(PARTS):
                    lanes = pl.ds(pl.multiple_of(p * FEAT + 128 * r, 128), 128)
                    lhs[first : first + PATCH, lanes] = (centred[:, lanes] * mods[r : r + 1]).astype(BF16)
                    kept = jnp.where((sub == PARTS + r) | (sub == 2 * PARTS + r), mods, 0.0)
                    lhs[first + PATCH : first + own_rows, lanes] = kept.astype(BF16)

        found = jnp.dot(lhs[...], kv_weight[...], preferred_element_type=F32)
        for at, src in enumerate(sources):
            first = at * own_rows
            a_kv[src] = found[first : first + PATCH].astype(BF16)
            b_kv[src] = jnp.broadcast_to(
                jnp.sum(found[first + PATCH : first + own_rows], axis=0, keepdims=True), (8, 2 * HD)
            )

    def tokens(src, matrix, bias):
        blocks = xall[src].reshape(SEQ * XROWS, 128)
        zero = jnp.zeros_like(matrix)
        found = []
        for pair in ([matrix, zero], [zero, matrix]):
            wide = jnp.dot(blocks, jnp.concatenate(pair, axis=0), preferred_element_type=F32)
            wide = wide.reshape(SEQ, XROWS, wide.shape[1])[:, 0:HALF]
            found.append(wide.reshape(SEQ * HALF, wide.shape[2]) + bias)
        return found

    group = SEQ * HALF
    mine = slot_group[slot]

    def prepare(i):
        for at, own in enumerate((True, False)):
            src = x.source(i, own)
            b = lax.rem(src + 1, SLOTS)
            keep = jnp.full((1, HD), group_mask[mine, slot_group[b]], jnp.int32).astype(F32)
            for half, t in enumerate(tokens(src, a_kv[b], b_kv[b][0:1])):
                rows = slice((2 * at + half) * group, (2 * at + half + 1) * group)
                keys[rows, :] = unit(t[:, 0:HD]).astype(BF16)
                values[rows, 0:HD] = (t[:, HD : 2 * HD] * keep).astype(BF16)
                values[rows, HD : 2 * HD] = jnp.broadcast_to(keep, (group, HD)).astype(BF16)

    def attend(i):
        prepare(i)
        scores = lax.dot_general(q_ref[...], keys[...], NT, preferred_element_type=F32)
        probs = jnp.exp2(scores).astype(BF16)
        total[...] += jnp.dot(probs, values[...], preferred_element_type=F32)

    total[...] = jnp.zeros_like(total)
    for i in range(PAIRS):
        m.first(i)
    for i in range(2):
        x.first(i)
    for i in range(4):
        m.second(i)
    for i in range(2, 4):
        x.first(i)
    for i in range(4, 8):
        m.second(i)
    for i in range(4, 6):
        x.first(i)
    for i in range(2):
        x.second(i)
    for i in range(8):
        m.third(i)
    for i in range(6, 8):
        x.first(i)
    for i in range(2, 4):
        x.second(i)
    for i in range(8):
        m.fourth(i)

    @pl.loop(0, PAIRS // 2)
    def _(k):
        build(k)

    for i in range(2):
        x.third(i)
    for i in range(4, 8):
        x.second(i)
    for i in range(2, 8):
        x.third(i)
    for i in range(2):
        x.fourth(i)
    scale = 1.0 / (math.sqrt(HD) * math.log(2.0))
    for half, t in enumerate(tokens(lax.rem(slot + SLOTS - 1, SLOTS), a_q.astype(BF16), b_q)):
        q_ref[half * group : half * group + group, :] = (unit(t) * scale).astype(BF16)

    @pl.loop(0, PAIRS)
    def _(i):
        @pl.when(i >= 2)
        def _():
            x.fourth(i)

        attend(i)

    for p in range(SEQ):
        found = []
        for half in range(2):
            rows = slice(half * group + p * HALF, half * group + p * HALF + HALF)
            found.append(total[rows, 0:HD] / total[rows, HD : 2 * HD])
        attn[p * TOK : p * TOK + TOK, :] = jnp.concatenate(found, axis=0).astype(attn.dtype)
    attn_copy = pltpu.make_async_copy(attn, attn_out, local_sem.at[1])
    attn_copy.start()
    for copy in sends:
        copy.wait_send()
    m.finish()
    x.finish()
    stepped_copy.wait()
    attn_copy.wait()


def spread_sems():
    dma = pltpu.SemaphoreType.DMA
    return [dma((SLOTS,)) for _ in range(8)]


def local(
    hidden,
    final_mod,
    head_weight,
    latents,
    fresh_noise,
    step_index,
    slot_group,
    group_mask,
    patch_weight,
    block_mod,
    qkv_weight,
):
    hbm = pl.BlockSpec(memory_space=pl.ANY)
    dma = pltpu.SemaphoreType.DMA
    vmem = pltpu.VMEM
    smem = pltpu.SMEM
    stepped_t, attn = pl.pallas_call(
        kernel,
        out_shape=(
            jax.ShapeDtypeStruct((PATCH, TOK), F32),
            jax.ShapeDtypeStruct((SEQ * TOK, HD), BF16),
        ),
        in_specs=[hbm] * 11,
        out_specs=(hbm, hbm),
        scratch_shapes=[
            vmem((TOK, D // HEADS), BF16),
            vmem((1, 2, D // HEADS), F32),
            vmem((PATCH, D // HEADS), F32),
            vmem((PATCH, TOK), F32),
            vmem((PATCH, TOK), F32),
            smem((SLOTS,), jnp.int32),
            smem((SLOTS,), jnp.int32),
            smem((SLOTS, SLOTS), jnp.int32),
            vmem((PATCH, D), BF16),
            vmem((1, 2, D), F32),
            vmem((D, HD), BF16),
            vmem((D, 2 * HD), BF16),
            vmem((PATCH, TOK), F32),
            vmem((SEQ * TOK, HD), BF16),
            vmem((SLOTS, SEQ, XROWS, 128), BF16),
            vmem((SLOTS, SEQ, MROWS, 128), BF16),
            vmem((TOK, 128), F32),
            vmem((HEADS - 1, TOK, 128), F32),
            vmem((PATCH, D), F32),
            vmem((4 * (PATCH + MROWS), D), BF16),
            vmem((SLOTS, PATCH, 2 * HD), BF16),
            vmem((SLOTS, 8, 2 * HD), F32),
            vmem((SEQ * TOK, HD), BF16),
            vmem((KEYS, HD), BF16),
            vmem((KEYS, 2 * HD), BF16),
            vmem((SEQ * TOK, 2 * HD), F32),
            dma((13,)),
            dma((HEADS - 1,)),
            dma((HEADS - 1,)),
        ]
        + spread_sems()
        + spread_sems(),
        compiler_params=pltpu.CompilerParams(
            collective_id=0, has_side_effects=True, vmem_limit_bytes=56 * 2**20
        ),
        name="window",
    )(
        hidden,
        final_mod,
        head_weight.T,
        latents.T,
        fresh_noise.T,
        step_index,
        slot_group,
        group_mask,
        patch_weight,
        block_mod,
        jnp.transpose(qkv_weight, (1, 0, 2)),
    )
    return stepped_t.T, attn


def solution(mesh):
    in_specs = (
        P(("slot", "seq"), "head"),
        P("slot", None, "head"),
        P("head", None),
        P(("slot", "seq"), None),
        P("seq", None),
        P(),
        P(),
        P(),
        P(),
        P("slot", None, None),
        P(None, None, ("seq", "head")),
    )
    out_specs = (P(("slot", "seq"), None), P("slot", ("seq", "head")))
    return jax.shard_map(local, mesh=mesh, in_specs=in_specs, out_specs=out_specs, check_vma=False)
```

time: 77.6 us -> 66.2 us (0.85); the launches traced: 76.5 us -> 66 us
  local copies, waits for them, and re-layouts: 9.68 us -> 2.97 us
  Pallas kernels: 66.1 us -> 62.4 us
    unnamed x23 -> x2, local copies, waits for them, and re-layouts: 9.68 us -> 2.97 us
    pallas_call x2 -> x1, Pallas kernels: 66.1 us -> 62.4 us  [local(): pl.pallas_call(kernel, out_shape=(jax.ShapeDtypeStruct((PATCH, TOK), F32)...]
where the time goes in v2:
time: 66.2 us; the launch traced here: 66 us
  Pallas kernels  62.4 us (94%)
  local copies, waits for them, and re-layouts  2.97 us (4%)
    pallas_call x1, Pallas kernels, local(): pl.pallas_call(kernel, out_shape=(jax.ShapeDtypeStruct((PATCH, TOK), F32)...  62.4 us
    unnamed x2, local copies, waits for them, and re-layouts  2.97 us

profile of v2, /device:TPU:1, one launch (start us, length us, event | category | flops | bytes accessed | tf_op | source)
XLA Modules:
  0.0 66.0 jit_solution(16053737706006206019)
XLA Ops:
  0.6 62.4 %window.1 = (f32[64,80]{1,0:T(8,128)}, bf16[640,128]{1,0:T(8,128)(2,1)}) custom-call(bf16[80,1280]{1,0:T(8,128)(2,1)} %hidden_in.1, f32[1,2,1280]{2,1,0:T(2,128)} %final_mod_in.1, f32[64,1280]{1,0:T(8,128)} %bitcast.6, f32[64,80]{1,0:T(8,128)} %bitcast.7, f32[64,80]{1,0:T(8,128)} %bitcast.8, s32[16]{0:T(128)} %step_in.1, s32[16]{0:T(128)} %group_in.1, ...), custom_call_target="tpu_custom_call" | custom-call | tf_op jit(solution)/shard_map/window/pallas_call | solution.py:504
  63.0 1.4 %copy.15 = f32[80,64]{0,1:T(8,128)} copy(f32[80,64]{0,1:T(8,128)} %bitcast.9) | data formatting | bytes 40960
  64.4 1.6 %copy.16 = bf16[640,128]{1,0:T(8,128)(2,1)} copy(bf16[640,128]{1,0:T(8,128)(2,1)} %get-tuple-element.9) | data formatting | bytes 327680

commit v3 on v2

--- a/solution.py
+++ b/solution.py
@@ -78,9 +78,8 @@
     def slot_send(self):
         @pl.when(self.own)
         def _():
-            @pl.loop(1, SLOTS)
-            def _(k):
-                self.slot_copy(k).start()
+            for k in range(1, SLOTS):
+                self.slot_copy(k // 2 if k % 2 == 0 else SLOTS - (k + 1) // 2).start()
 
     def slot_wait(self, i):
         src = self.source(i)
@@ -170,27 +169,30 @@
     stack = jnp.concatenate(split(gained, 3), axis=0)
     parts = lax.dot_general(h, stack, NT, preferred_element_type=F32)
     part = parts[:, 0:PATCH] + parts[:, PATCH : 2 * PATCH] + parts[:, 2 * PATCH : 3 * PATCH]
-    lane = lax.broadcasted_iota(jnp.int32, (TOK, PATCH), 1)
+    lane = lax.broadcasted_iota(jnp.int32, (TOK, 128), 1)
     pad = jnp.zeros((TOK - PATCH, 1), F32)
     gain_sum = jnp.concatenate([gain_sum, pad], axis=0)
     shift_sum = jnp.concatenate([shift_sum, pad], axis=0)
     stats = jnp.where(lane == 0, mean, jnp.where(lane == 1, spread, 0.0))
     stats = jnp.where(lane == 2, gain_sum, jnp.where(lane == 3, shift_sum, stats))
-    msg[...] = jnp.concatenate([part, stats], axis=1)
+    stats = jnp.transpose(jnp.concatenate([stats, jnp.zeros((128 - TOK, 128), F32)], axis=0))
+    msg[0:HALF, :] = jnp.concatenate([part[0:HALF], part[HALF:TOK]], axis=1)
+    msg[HALF:XROWS, :] = stats[0:8]
 
 
 def whole_velocity(parts, count):
     total = sum(parts)
-    mean = total[:, PATCH : PATCH + 1] / len(parts)
-    spread = total[:, PATCH + 1 : PATCH + 2]
+    mean = total[HALF : HALF + 1] / len(parts)
+    spread = total[HALF + 1 : HALF + 2]
     for p in parts:
-        off = p[:, PATCH : PATCH + 1] - mean
+        off = p[HALF : HALF + 1] - mean
         spread = spread + count * off * off
-    turned = jnp.transpose(jnp.concatenate([total, jnp.zeros((128 - TOK, 128), F32)], axis=0))
-    gain_row = turned[PATCH + 2 : PATCH + 3, 0:PATCH]
-    shift_row = turned[PATCH + 3 : PATCH + 4, 0:PATCH]
     scale = lax.rsqrt(spread / (count * len(parts)) + EPS)
-    return (total[:, 0:PATCH] - mean * gain_row) * scale + shift_row
+    turned = jnp.transpose(jnp.concatenate([mean, scale, jnp.zeros((126, 128), F32)], axis=0))[0:TOK]
+    gain_row = total[HALF + 2 : HALF + 3, 0:PATCH]
+    shift_row = total[HALF + 3 : HALF + 4, 0:PATCH]
+    product = jnp.concatenate([total[0:HALF, 0:PATCH], total[0:HALF, PATCH:128]], axis=0)
+    return (product - turned[:, 0:1] * gain_row) * turned[:, 1:2] + shift_row
 
 
 def sigma_of(level):
@@ -239,8 +241,10 @@
     a_kv,
     b_kv,
     q_ref,
-    keys,
-    values,
+    keys_a,
+    values_a,
+    keys_b,
+    values_b,
     total,
     local_sem,
     ps,
@@ -368,11 +372,10 @@
         for at, src in enumerate(sources):
             first = at * own_rows
 
-            @pl.loop(0, SEQ)
-            def _(p):
+            for p in range(SEQ):
                 mods = mall[src, p].astype(F32)
                 for r in range(PARTS):
-                    lanes = pl.ds(pl.multiple_of(p * FEAT + 128 * r, 128), 128)
+                    lanes = slice(p * FEAT + 128 * r, p * FEAT + 128 * r + 128)
                     lhs[first : first + PATCH, lanes] = (centred[:, lanes] * mods[r : r + 1]).astype(BF16)
                     kept = jnp.where((sub == PARTS + r) | (sub == 2 * PARTS + r), mods, 0.0)
                     lhs[first + PATCH : first + own_rows, lanes] = kept.astype(BF16)
@@ -395,10 +398,11 @@
             found.append(wide.reshape(SEQ * HALF, wide.shape[2]) + bias)
         return found
 
+    pairs = ((keys_a, values_a), (keys_b, values_b))
     group = SEQ * HALF
     mine = slot_group[slot]
 
-    def prepare(i):
+    def prepare(i, keys, values):
         for at, own in enumerate((True, False)):
             src = x.source(i, own)
             b = lax.rem(src + 1, SLOTS)
@@ -410,57 +414,53 @@
                 values[rows, HD : 2 * HD] = jnp.broadcast_to(keep, (group, HD)).astype(BF16)
 
     def attend(i):
-        prepare(i)
+        keys, values = pairs[i % 2]
+        prepare(i, keys, values)
         scores = lax.dot_general(q_ref[...], keys[...], NT, preferred_element_type=F32)
         probs = jnp.exp2(scores).astype(BF16)
         total[...] += jnp.dot(probs, values[...], preferred_element_type=F32)
 
     total[...] = jnp.zeros_like(total)
-    for i in range(PAIRS):
-        m.first(i)
-    for i in range(2):
-        x.first(i)
-    for i in range(4):
-        m.second(i)
-    for i in range(2, 4):
-        x.first(i)
-    for i in range(4, 8):
-        m.second(i)
-    for i in range(4, 6):
-        x.first(i)
-    for i in range(2):
-        x.second(i)
-    for i in range(8):
-        m.third(i)
-    for i in range(6, 8):
-        x.first(i)
-    for i in range(2, 4):
-        x.second(i)
-    for i in range(8):
-        m.fourth(i)
-
-    @pl.loop(0, PAIRS // 2)
-    def _(k):
-        build(k)
-
-    for i in range(2):
-        x.third(i)
-    for i in range(4, 8):
-        x.second(i)
-    for i in range(2, 8):
-        x.third(i)
-    for i in range(2):
+    def queries():
+        scale = 1.0 / (math.sqrt(HD) * math.log(2.0))
+        for half, t in enumerate(tokens(lax.rem(slot + SLOTS - 1, SLOTS), a_q.astype(BF16), b_q)):
+            q_ref[half * group : half * group + group, :] = (unit(t) * scale).astype(BF16)
+
+    def run(what, first, last):
+        for i in range(first, last + 1):
+            what(i)
+
+    run(m.first, 0, 7)
+    run(x.first, 0, 1)
+    run(m.second, 0, 3)
+    run(x.first, 2, 3)
+    run(m.second, 4, 7)
+    run(x.first, 4, 5)
+    run(m.third, 0, 3)
+    run(x.first, 6, 7)
+    run(x.second, 0, 1)
+    run(m.fourth, 0, 1)
+    build(0)
+    run(m.third, 4, 7)
+    run(x.second, 2, 3)
+    run(m.fourth, 2, 3)
+    build(1)
+    run(x.third, 0, 1)
+    run(x.second, 4, 5)
+    run(m.fourth, 4, 5)
+    build(2)
+    run(x.second, 6, 7)
+    run(x.third, 2, 3)
+    run(m.fourth, 6, 7)
+    build(3)
+    run(x.fourth, 0, 1)
+    queries()
+    attend(0)
+    run(x.third, 4, 5)
+    attend(1)
+    run(x.third, 6, 7)
+    for i in range(2, PAIRS):
         x.fourth(i)
-    scale = 1.0 / (math.sqrt(HD) * math.log(2.0))
-    for half, t in enumerate(tokens(lax.rem(slot + SLOTS - 1, SLOTS), a_q.astype(BF16), b_q)):
-        q_ref[half * group : half * group + group, :] = (unit(t) * scale).astype(BF16)
-
-    @pl.loop(0, PAIRS)
-    def _(i):
-        @pl.when(i >= 2)
-        def _():
-            x.fourth(i)
-
         attend(i)
 
     for p in range(SEQ):
@@ -526,13 +526,15 @@
             vmem((SEQ * TOK, HD), BF16),
             vmem((SLOTS, SEQ, XROWS, 128), BF16),
             vmem((SLOTS, SEQ, MROWS, 128), BF16),
-            vmem((TOK, 128), F32),
-            vmem((HEADS - 1, TOK, 128), F32),
+            vmem((XROWS, 128), F32),
+            vmem((HEADS - 1, XROWS, 128), F32),
             vmem((PATCH, D), F32),
             vmem((4 * (PATCH + MROWS), D), BF16),
             vmem((SLOTS, PATCH, 2 * HD), BF16),
             vmem((SLOTS, 8, 2 * HD), F32),
             vmem((SEQ * TOK, HD), BF16),
+            vmem((KEYS, HD), BF16),
+            vmem((KEYS, 2 * HD), BF16),
             vmem((KEYS, HD), BF16),
             vmem((KEYS, 2 * HD), BF16),
             vmem((SEQ * TOK, 2 * HD), F32),

time: 66.2 us -> 59.5 us (0.90)
  Pallas kernels: 62.4 us -> 55.7 us
    pallas_call x1, Pallas kernels: 62.4 us -> 55.7 us  [local(): pl.pallas_call(kernel, out_shape=(jax.ShapeDtypeStruct((PATCH, TOK), F32)...]
where the time goes in v3:
time: 59.5 us; the launch traced here: 59.3 us
  Pallas kernels  55.7 us (94%)
  local copies, waits for them, and re-layouts  2.97 us (5%)
  between operations  0.64 us (1%)
    pallas_call x1, Pallas kernels, local(): pl.pallas_call(kernel, out_shape=(jax.ShapeDtypeStruct((PATCH, TOK), F32)...  55.7 us
    unnamed x2, local copies, waits for them, and re-layouts  2.97 us

profile of v3, /device:TPU:1, one launch (start us, length us, event | category | flops | bytes accessed | tf_op | source)
XLA Modules:
  0.0 59.3 jit_solution(810293409977163807)
XLA Ops:
  0.6 55.7 %window.1 = (f32[64,80]{1,0:T(8,128)}, bf16[640,128]{1,0:T(8,128)(2,1)}) custom-call(bf16[80,1280]{1,0:T(8,128)(2,1)} %hidden_in.1, f32[1,2,1280]{2,1,0:T(2,128)} %final_mod_in.1, f32[64,1280]{1,0:T(8,128)} %bitcast.6, f32[64,80]{1,0:T(8,128)} %bitcast.7, f32[64,80]{1,0:T(8,128)} %bitcast.8, s32[16]{0:T(128)} %step_in.1, s32[16]{0:T(128)} %group_in.1, ...), custom_call_target="tpu_custom_call" | custom-call | tf_op jit(solution)/shard_map/window/pallas_call | solution.py:504
  56.3 1.4 %copy.15 = f32[80,64]{0,1:T(8,128)} copy(f32[80,64]{0,1:T(8,128)} %bitcast.9) | data formatting | bytes 40960
  57.7 1.6 %copy.16 = bf16[640,128]{1,0:T(8,128)(2,1)} copy(bf16[640,128]{1,0:T(8,128)(2,1)} %get-tuple-element.9) | data formatting | bytes 327680

commit v4 on v3

--- a/solution.py
+++ b/solution.py
@@ -44,8 +44,9 @@
 
 
 class Spread:
-    def __init__(self, buf, shift, sems):
+    def __init__(self, buf, shift, direct, sems):
         self.buf = buf
+        self.direct = direct
         self.zs, self.zr, self.qs, self.qr, self.ys, self.yr, self.cs, self.cr = sems
         self.shift = shift
         self.slot = lax.axis_index("slot")
@@ -60,7 +61,7 @@
     def source(self, i, mine=True):
         odd = lax.rem(i, 2) == 1
         even_list = jnp.where(odd, i + 1, SLOTS - i)
-        odd_list = jnp.where(odd, SLOTS - i, i + 1)
+        odd_list = jnp.where(odd, i, SLOTS - 1 - i)
         if self.shift:
             even_list, odd_list = odd_list + 1, even_list + 1
         near = jnp.where(self.own, even_list, odd_list) if mine else jnp.where(self.own, odd_list, even_list)
@@ -92,12 +93,13 @@
     def row_send(self, i):
         src = self.source(i)
         block = self.buf.at[src, self.seq]
-        for k in range(1, ROW):
-            to = self.low * ROW + lax.rem(self.at + k, ROW)
+        peers = SEQ if self.direct else ROW
+        for k in range(1, peers):
+            to = lax.rem(self.seq + k, SEQ) if self.direct else self.low * ROW + lax.rem(self.at + k, ROW)
             remote(block, block, self.qs.at[src], self.qr.at[src], {"seq": to}).start()
 
     def row_all(self, src):
-        blocks = self.buf.at[src, pl.ds(0, ROW - 1)]
+        blocks = self.buf.at[src, pl.ds(0, (SEQ if self.direct else ROW) - 1)]
         return remote(blocks, blocks, self.qs.at[src], self.qr.at[src], {"seq": self.seq})
 
     def side_copy(self, i):
@@ -122,6 +124,9 @@
     def second(self, i):
         src = self.source(i)
         self.row_all(src).wait_recv()
+        if self.direct:
+            self.core_all(src).start()
+            return
         self.side_copy(i).start()
         self.core_copy(src, self.low).start()
 
@@ -144,7 +149,8 @@
         def _(i):
             src = self.source(i)
             self.row_all(src).wait_send()
-            self.side_copy(i).wait_send()
+            if not self.direct:
+                self.side_copy(i).wait_send()
             self.core_all(src).wait_send()
 
 
@@ -251,8 +257,8 @@
     pr,
     *sems,
 ):
-    x = Spread(xall, 0, sems[:8])
-    m = Spread(mall, 1, sems[8:])
+    x = Spread(xall, 0, False, sems[:8])
+    m = Spread(mall, 1, True, sems[8:])
     slot, seq, head = x.slot, x.seq, x.head
     loads = [
         pltpu.make_async_copy(src, dst, local_sem.at[i])
@@ -285,10 +291,9 @@
         greet({"slot": lax.rem(slot + k, SLOTS)})
     for k in range(1, HEADS):
         greet({"head": lax.rem(head + k, HEADS)})
-    for k in range(1, ROW):
-        greet({"seq": x.low * ROW + lax.rem(x.at + k, ROW)})
+    for k in range(1, SEQ):
+        greet({"seq": lax.rem(seq + k, SEQ)})
     side = (1 - x.low) * ROW + x.at
-    greet({"seq": side})
     greet({"seq": side, "head": lax.rem(head + 2, HEADS)})
 
     for copy in loads[:4]:
@@ -307,7 +312,7 @@
         rows += [jnp.zeros((1, 128), F32)]
         mall[slot, seq] = jnp.concatenate(rows, axis=0).astype(BF16)
 
-    pl.semaphore_wait(barrier, SLOTS + HEADS + ROW - 3 + 2)
+    pl.semaphore_wait(barrier, SLOTS + HEADS + SEQ - 3 + 1)
     sends = [
         remote(msg, got.at[k - 1], ps.at[k - 1], pr.at[k - 1], {"head": lax.rem(head + k, HEADS)})
         for k in range(1, HEADS)
@@ -402,20 +407,20 @@
     group = SEQ * HALF
     mine = slot_group[slot]
 
-    def prepare(i, keys, values):
-        for at, own in enumerate((True, False)):
-            src = x.source(i, own)
-            b = lax.rem(src + 1, SLOTS)
-            keep = jnp.full((1, HD), group_mask[mine, slot_group[b]], jnp.int32).astype(F32)
-            for half, t in enumerate(tokens(src, a_kv[b], b_kv[b][0:1])):
-                rows = slice((2 * at + half) * group, (2 * at + half + 1) * group)
-                keys[rows, :] = unit(t[:, 0:HD]).astype(BF16)
-                values[rows, 0:HD] = (t[:, HD : 2 * HD] * keep).astype(BF16)
-                values[rows, HD : 2 * HD] = jnp.broadcast_to(keep, (group, HD)).astype(BF16)
+    def prepare(i, own):
+        keys, values = pairs[i % 2]
+        src = x.source(i, own)
+        b = lax.rem(src + 1, SLOTS)
+        keep = jnp.full((1, HD), group_mask[mine, slot_group[b]], jnp.int32).astype(F32)
+        for half, t in enumerate(tokens(src, a_kv[b], b_kv[b][0:1])):
+            first = (half if own else 2 + half) * group
+            rows = slice(first, first + group)
+            keys[rows, :] = unit(t[:, 0:HD]).astype(BF16)
+            values[rows, 0:HD] = (t[:, HD : 2 * HD] * keep).astype(BF16)
+            values[rows, HD : 2 * HD] = jnp.broadcast_to(keep, (group, HD)).astype(BF16)
 
     def attend(i):
         keys, values = pairs[i % 2]
-        prepare(i, keys, values)
         scores = lax.dot_general(q_ref[...], keys[...], NT, preferred_element_type=F32)
         probs = jnp.exp2(scores).astype(BF16)
         total[...] += jnp.dot(probs, values[...], preferred_element_type=F32)
@@ -432,35 +437,37 @@
 
     run(m.first, 0, 7)
     run(x.first, 0, 1)
-    run(m.second, 0, 3)
+    run(m.second, 0, 1)
     run(x.first, 2, 3)
-    run(m.second, 4, 7)
-    run(x.first, 4, 5)
-    run(m.third, 0, 3)
-    run(x.first, 6, 7)
-    run(x.second, 0, 1)
+    run(m.second, 2, 3)
     run(m.fourth, 0, 1)
     build(0)
-    run(m.third, 4, 7)
-    run(x.second, 2, 3)
+    run(x.first, 4, 5)
+    run(m.second, 4, 5)
     run(m.fourth, 2, 3)
     build(1)
-    run(x.third, 0, 1)
-    run(x.second, 4, 5)
+    run(x.first, 6, 6)
+    run(x.second, 0, 0)
+    run(m.second, 6, 7)
     run(m.fourth, 4, 5)
+    run(x.first, 7, 7)
     build(2)
-    run(x.second, 6, 7)
-    run(x.third, 2, 3)
+    run(x.second, 1, 2)
     run(m.fourth, 6, 7)
     build(3)
-    run(x.fourth, 0, 1)
+    run(x.third, 0, 0)
+    run(x.second, 3, 3)
+    run(x.fourth, 0, 0)
     queries()
-    attend(0)
-    run(x.third, 4, 5)
-    attend(1)
-    run(x.third, 6, 7)
-    for i in range(2, PAIRS):
-        x.fourth(i)
+    for i in range(PAIRS):
+        if i + 4 < PAIRS:
+            x.second(i + 4)
+        if i + 1 < PAIRS:
+            x.third(i + 1)
+        prepare(i, True)
+        if i > 0:
+            x.fourth(i)
+        prepare(i, False)
         attend(i)
 
     for p in range(SEQ):

time: 59.5 us -> 59 us (level)
  no operation moved by 1% of the time
where the time goes in v4:
time: 59 us; the launch traced here: 58.8 us
  Pallas kernels  55.2 us (94%)
  local copies, waits for them, and re-layouts  2.97 us (5%)
  between operations  0.64 us (1%)
    pallas_call x1, Pallas kernels, local(): pl.pallas_call(kernel, out_shape=(jax.ShapeDtypeStruct((PATCH, TOK), F32)...  55.2 us
    unnamed x2, local copies, waits for them, and re-layouts  2.97 us

profile of v4, /device:TPU:1, one launch (start us, length us, event | category | flops | bytes accessed | tf_op | source)
XLA Modules:
  0.0 58.8 jit_solution(3639048935505195524)
XLA Ops:
  0.6 55.2 %window.1 = (f32[64,80]{1,0:T(8,128)}, bf16[640,128]{1,0:T(8,128)(2,1)}) custom-call(bf16[80,1280]{1,0:T(8,128)(2,1)} %hidden_in.1, f32[1,2,1280]{2,1,0:T(2,128)} %final_mod_in.1, f32[64,1280]{1,0:T(8,128)} %bitcast.6, f32[64,80]{1,0:T(8,128)} %bitcast.7, f32[64,80]{1,0:T(8,128)} %bitcast.8, s32[16]{0:T(128)} %step_in.1, s32[16]{0:T(128)} %group_in.1, ...), custom_call_target="tpu_custom_call" | custom-call | tf_op jit(solution)/shard_map/window/pallas_call | solution.py:511
  55.8 1.4 %copy.15 = f32[80,64]{0,1:T(8,128)} copy(f32[80,64]{0,1:T(8,128)} %bitcast.9) | data formatting | bytes 40960
  57.2 1.6 %copy.16 = bf16[640,128]{1,0:T(8,128)(2,1)} copy(bf16[640,128]{1,0:T(8,128)(2,1)} %get-tuple-element.9) | data formatting | bytes 327680

commit v5 on v4

--- a/solution.py
+++ b/solution.py
@@ -28,6 +28,18 @@
 NT = (((1,), (1,)), ((), ()))
 PAIRS = SLOTS // 2
 ROW = SEQ // 2
+RELAYED = 8
+ORDER = (
+    ("mf", 0), ("mf", 1), ("mf", 2), ("mf", 3), ("mf", 4), ("mf", 5), ("xf", 0), ("xf", 1), ("ms", 0),
+    ("ms", 1), ("mf", 6), ("mf", 7), ("xf", 2), ("xf", 3), ("ms", 2), ("ms", 3), ("mh", 0), ("mh", 1),
+    ("B", 0), ("xf", 4), ("xf", 5), ("ms", 4), ("ms", 5), ("mh", 2), ("mh", 3), ("xs", 0), ("xs", 1),
+    ("B", 1), ("xf", 6), ("xf", 7), ("xs", 2), ("xs", 3), ("ms", 6), ("ms", 7), ("mh", 4), ("mh", 5),
+    ("B", 2), ("xs", 4), ("mh", 6), ("mh", 7), ("xt", 0), ("xt", 1), ("B", 3), ("xs", 5), ("xh", 0),
+    ("Q", 0), ("P", 0), ("xs", 6), ("xs", 7), ("xt", 2), ("xt", 3), ("xh", 1), ("P", 1), ("A", 0),
+    ("xt", 4), ("xt", 5), ("xh", 2), ("P", 2), ("A", 1), ("xt", 6), ("xt", 7), ("xh", 3), ("P", 3),
+    ("A", 2), ("xh", 4), ("P", 4), ("A", 3), ("xh", 5), ("P", 5), ("A", 4), ("xh", 6), ("P", 6),
+    ("A", 5), ("xh", 7), ("P", 7), ("A", 6), ("A", 7),
+)
 PARTS = FEAT // 128
 KEYS = 2 * SEQ * TOK
 
@@ -44,9 +56,9 @@
 
 
 class Spread:
-    def __init__(self, buf, shift, direct, sems):
+    def __init__(self, buf, shift, relayed, sems):
         self.buf = buf
-        self.direct = direct
+        self.relayed = relayed
         self.zs, self.zr, self.qs, self.qr, self.ys, self.yr, self.cs, self.cr = sems
         self.shift = shift
         self.slot = lax.axis_index("slot")
@@ -93,13 +105,14 @@
     def row_send(self, i):
         src = self.source(i)
         block = self.buf.at[src, self.seq]
-        peers = SEQ if self.direct else ROW
-        for k in range(1, peers):
-            to = lax.rem(self.seq + k, SEQ) if self.direct else self.low * ROW + lax.rem(self.at + k, ROW)
+        relay = i < self.relayed
+        for k in range(1, ROW if relay else SEQ):
+            to = self.low * ROW + lax.rem(self.at + k, ROW) if relay else lax.rem(self.seq + k, SEQ)
             remote(block, block, self.qs.at[src], self.qr.at[src], {"seq": to}).start()
 
-    def row_all(self, src):
-        blocks = self.buf.at[src, pl.ds(0, (SEQ if self.direct else ROW) - 1)]
+    def row_all(self, i):
+        src = self.source(i)
+        blocks = self.buf.at[src, pl.ds(0, (ROW if i < self.relayed else SEQ) - 1)]
         return remote(blocks, blocks, self.qs.at[src], self.qr.at[src], {"seq": self.seq})
 
     def side_copy(self, i):
@@ -123,14 +136,16 @@
 
     def second(self, i):
         src = self.source(i)
-        self.row_all(src).wait_recv()
-        if self.direct:
+        self.row_all(i).wait_recv()
+        if i >= self.relayed:
             self.core_all(src).start()
             return
         self.side_copy(i).start()
         self.core_copy(src, self.low).start()
 
     def third(self, i):
+        if i >= self.relayed:
+            return
         src = self.source(i)
         self.side_copy(i).wait_recv()
         self.core_copy(src, 1 - self.low).start()
@@ -145,13 +160,11 @@
             def _(k):
                 self.slot_copy(k).wait_send()
 
-        @pl.loop(0, PAIRS)
-        def _(i):
-            src = self.source(i)
-            self.row_all(src).wait_send()
-            if not self.direct:
+        for i in range(PAIRS):
+            self.row_all(i).wait_send()
+            if i < self.relayed:
                 self.side_copy(i).wait_send()
-            self.core_all(src).wait_send()
+            self.core_all(self.source(i)).wait_send()
 
 
 def split(value, count):
@@ -257,8 +270,8 @@
     pr,
     *sems,
 ):
-    x = Spread(xall, 0, False, sems[:8])
-    m = Spread(mall, 1, True, sems[8:])
+    x = Spread(xall, 0, RELAYED, sems[:8])
+    m = Spread(mall, 1, 0, sems[8:])
     slot, seq, head = x.slot, x.seq, x.head
     loads = [
         pltpu.make_async_copy(src, dst, local_sem.at[i])
@@ -419,6 +432,10 @@
             values[rows, 0:HD] = (t[:, HD : 2 * HD] * keep).astype(BF16)
             values[rows, HD : 2 * HD] = jnp.broadcast_to(keep, (group, HD)).astype(BF16)
 
+    def pair(i):
+        prepare(i, True)
+        prepare(i, False)
+
     def attend(i):
         keys, values = pairs[i % 2]
         scores = lax.dot_general(q_ref[...], keys[...], NT, preferred_element_type=F32)
@@ -435,41 +452,23 @@
         for i in range(first, last + 1):
             what(i)
 
-    run(m.first, 0, 7)
-    run(x.first, 0, 1)
-    run(m.second, 0, 1)
-    run(x.first, 2, 3)
-    run(m.second, 2, 3)
-    run(m.fourth, 0, 1)
-    build(0)
-    run(x.first, 4, 5)
-    run(m.second, 4, 5)
-    run(m.fourth, 2, 3)
-    build(1)
-    run(x.first, 6, 6)
-    run(x.second, 0, 0)
-    run(m.second, 6, 7)
-    run(m.fourth, 4, 5)
-    run(x.first, 7, 7)
-    build(2)
-    run(x.second, 1, 2)
-    run(m.fourth, 6, 7)
-    build(3)
-    run(x.third, 0, 0)
-    run(x.second, 3, 3)
-    run(x.fourth, 0, 0)
-    queries()
-    for i in range(PAIRS):
-        if i + 4 < PAIRS:
-            x.second(i + 4)
-        if i + 1 < PAIRS:
-            x.third(i + 1)
-        prepare(i, True)
-        if i > 0:
-            x.fourth(i)
-        prepare(i, False)
-        attend(i)
-
+    steps = {
+        "mf": m.first,
+        "ms": m.second,
+        "mh": m.fourth,
+        "xf": x.first,
+        "xs": x.second,
+        "xt": x.third,
+        "xh": x.fourth,
+        "B": build,
+        "P": pair,
+        "A": attend,
+    }
+    for what, i in ORDER:
+        if what == "Q":
+            queries()
+        else:
+            steps[what](i)
     for p in range(SEQ):
         found = []
         for half in range(2):

time: 59 us -> 55.2 us (0.936)
  Pallas kernels: 55.2 us -> 51.4 us
    pallas_call x1, Pallas kernels: 55.2 us -> 51.4 us  [local(): pl.pallas_call(kernel, out_shape=(jax.ShapeDtypeStruct((PATCH, TOK), F32)...]
where the time goes in v5:
time: 55.2 us; the launch traced here: 55 us
  Pallas kernels  51.4 us (93%)
  local copies, waits for them, and re-layouts  2.97 us (5%)
  between operations  0.64 us (1%)
    pallas_call x1, Pallas kernels, local(): pl.pallas_call(kernel, out_shape=(jax.ShapeDtypeStruct((PATCH, TOK), F32)...  51.4 us
    unnamed x2, local copies, waits for them, and re-layouts  2.97 us

profile of v5, /device:TPU:1, one launch (start us, length us, event | category | flops | bytes accessed | tf_op | source)
XLA Modules:
  0.0 55.0 jit_solution(15169228138534595932)
XLA Ops:
  0.6 51.4 %window.1 = (f32[64,80]{1,0:T(8,128)}, bf16[640,128]{1,0:T(8,128)(2,1)}) custom-call(bf16[80,1280]{1,0:T(8,128)(2,1)} %hidden_in.1, f32[1,2,1280]{2,1,0:T(2,128)} %final_mod_in.1, f32[64,1280]{1,0:T(8,128)} %bitcast.6, f32[64,80]{1,0:T(8,128)} %bitcast.7, f32[64,80]{1,0:T(8,128)} %bitcast.8, s32[16]{0:T(128)} %step_in.1, s32[16]{0:T(128)} %group_in.1, ...), custom_call_target="tpu_custom_call" | custom-call | tf_op jit(solution)/shard_map/window/pallas_call | solution.py:510
  52.1 1.4 %copy.15 = f32[80,64]{0,1:T(8,128)} copy(f32[80,64]{0,1:T(8,128)} %bitcast.9) | data formatting | bytes 40960
  53.4 1.6 %copy.16 = bf16[640,128]{1,0:T(8,128)(2,1)} copy(bf16[640,128]{1,0:T(8,128)(2,1)} %get-tuple-element.9) | data formatting | bytes 327680

commit v6 on v5

--- a/solution.py
+++ b/solution.py
@@ -28,17 +28,16 @@
 NT = (((1,), (1,)), ((), ()))
 PAIRS = SLOTS // 2
 ROW = SEQ // 2
-RELAYED = 8
+STEPS_EACH = 2
+RELAYED = 4
+MOD_RELAYED = 0
 ORDER = (
-    ("mf", 0), ("mf", 1), ("mf", 2), ("mf", 3), ("mf", 4), ("mf", 5), ("xf", 0), ("xf", 1), ("ms", 0),
-    ("ms", 1), ("mf", 6), ("mf", 7), ("xf", 2), ("xf", 3), ("ms", 2), ("ms", 3), ("mh", 0), ("mh", 1),
-    ("B", 0), ("xf", 4), ("xf", 5), ("ms", 4), ("ms", 5), ("mh", 2), ("mh", 3), ("xs", 0), ("xs", 1),
-    ("B", 1), ("xf", 6), ("xf", 7), ("xs", 2), ("xs", 3), ("ms", 6), ("ms", 7), ("mh", 4), ("mh", 5),
-    ("B", 2), ("xs", 4), ("mh", 6), ("mh", 7), ("xt", 0), ("xt", 1), ("B", 3), ("xs", 5), ("xh", 0),
-    ("Q", 0), ("P", 0), ("xs", 6), ("xs", 7), ("xt", 2), ("xt", 3), ("xh", 1), ("P", 1), ("A", 0),
-    ("xt", 4), ("xt", 5), ("xh", 2), ("P", 2), ("A", 1), ("xt", 6), ("xt", 7), ("xh", 3), ("P", 3),
-    ("A", 2), ("xh", 4), ("P", 4), ("A", 3), ("xh", 5), ("P", 5), ("A", 4), ("xh", 6), ("P", 6),
-    ("A", 5), ("xh", 7), ("P", 7), ("A", 6), ("A", 7),
+    ("mf", 0), ("mf", 1), ("mf", 2), ("xf", 0), ("ms", 0), ("mf", 3), ("xf", 1), ("ms", 1), ("mh", 0),
+    ("B", 0), ("xf", 2), ("ms", 2), ("mh", 1), ("xs", 0), ("B", 1), ("xf", 3), ("xs", 1), ("ms", 3),
+    ("mh", 2), ("B", 2), ("xs", 2), ("mh", 3), ("xt", 0), ("B", 3), ("xs", 3), ("xt", 1), ("xh", 0),
+    ("Q", 0), ("P", 0), ("P", 1), ("A", 0), ("xt", 2), ("xh", 1), ("P", 2), ("A", 1), ("xt", 3),
+    ("P", 3), ("A", 2), ("xh", 2), ("P", 4), ("A", 3), ("P", 5), ("A", 4), ("xh", 3), ("P", 6),
+    ("A", 5), ("P", 7), ("A", 6), ("A", 7),
 )
 PARTS = FEAT // 128
 KEYS = 2 * SEQ * TOK
@@ -55,37 +54,40 @@
     )
 
 
+def offset(odd, step):
+    if odd:
+        return step if step % 2 else SLOTS - 1 - step
+    return (step + 1 if step % 2 else SLOTS - step) % SLOTS
+
+
 class Spread:
-    def __init__(self, buf, shift, relayed, sems):
+    def __init__(self, buf, ahead, relayed, sems):
         self.buf = buf
         self.relayed = relayed
         self.zs, self.zr, self.qs, self.qr, self.ys, self.yr, self.cs, self.cr = sems
-        self.shift = shift
         self.slot = lax.axis_index("slot")
         self.seq = lax.axis_index("seq")
         self.head = lax.axis_index("head")
         self.core = lax.rem(self.head, 2)
         self.own = lax.rem(self.slot, 2) == self.core
+        self.mine = jnp.where(self.own, 0, 1)
         self.other_core = self.head + 1 - 2 * self.core
         self.low = self.seq // ROW
         self.at = lax.rem(self.seq, ROW)
-
-    def source(self, i, mine=True):
-        odd = lax.rem(i, 2) == 1
-        even_list = jnp.where(odd, i + 1, SLOTS - i)
-        odd_list = jnp.where(odd, i, SLOTS - 1 - i)
-        if self.shift:
-            even_list, odd_list = odd_list + 1, even_list + 1
-        near = jnp.where(self.own, even_list, odd_list) if mine else jnp.where(self.own, odd_list, even_list)
-        return lax.rem(self.slot + near, SLOTS)
-
-    def half(self, src, low):
-        return self.buf.at[src, pl.ds(low * ROW, ROW)]
+        self.place = {}
+        for odd in (0, 1):
+            for step in range(PAIRS):
+                far = (offset(1 - odd, step) + 1) % SLOTS if ahead else offset(odd, step)
+                self.place[far] = (odd, step)
 
     def slot_copy(self, k):
-        block = self.buf.at[self.slot, self.seq]
+        odd, step = self.place[SLOTS - k]
         return remote(
-            block, block, self.zs.at[k], self.zr.at[self.slot], {"slot": lax.rem(self.slot + k, SLOTS)}
+            self.buf.at[0, 0, self.seq],
+            self.buf.at[odd, step, self.seq],
+            self.zs.at[k],
+            self.zr.at[step],
+            {"slot": lax.rem(self.slot + k, SLOTS)},
         )
 
     def slot_send(self):
@@ -94,77 +96,74 @@
             for k in range(1, SLOTS):
                 self.slot_copy(k // 2 if k % 2 == 0 else SLOTS - (k + 1) // 2).start()
 
-    def slot_wait(self, i):
-        src = self.source(i)
-        block = self.buf.at[src, self.seq]
-
-        @pl.when(src != self.slot)
-        def _():
-            remote(block, block, self.zs.at[0], self.zr.at[src], {"slot": self.slot}).wait_recv()
-
-    def row_send(self, i):
-        src = self.source(i)
-        block = self.buf.at[src, self.seq]
-        relay = i < self.relayed
-        for k in range(1, ROW if relay else SEQ):
-            to = self.low * ROW + lax.rem(self.at + k, ROW) if relay else lax.rem(self.seq + k, SEQ)
-            remote(block, block, self.qs.at[src], self.qr.at[src], {"seq": to}).start()
-
-    def row_all(self, i):
-        src = self.source(i)
-        blocks = self.buf.at[src, pl.ds(0, (ROW if i < self.relayed else SEQ) - 1)]
-        return remote(blocks, blocks, self.qs.at[src], self.qr.at[src], {"seq": self.seq})
-
-    def side_copy(self, i):
-        src = self.source(i)
-        blocks = self.half(src, self.low)
-        head = lax.rem(self.head + 2 * lax.rem(i, 2), HEADS)
+    def slot_wait(self, step):
+        def wait():
+            block = self.buf.at[self.mine, step, self.seq]
+            remote(block, block, self.zs.at[0], self.zr.at[step], {"slot": self.slot}).wait_recv()
+
+        if step:
+            wait()
+        else:
+            pl.when(jnp.logical_not(self.own))(wait)
+
+    def blocks(self, g, seqs, mine=True):
+        steps = pl.ds(g * STEPS_EACH, STEPS_EACH)
+        return self.buf.at[self.mine if mine else 1 - self.mine, steps, seqs]
+
+    def copy(self, blocks, send, recv, g, device_id):
+        return remote(blocks, blocks, send.at[g], recv.at[g], device_id)
+
+    def row_copy(self, g, k):
+        relay = g < self.relayed
+        to = self.low * ROW + lax.rem(self.at + k, ROW) if relay else lax.rem(self.seq + k, SEQ)
+        return self.copy(self.blocks(g, self.seq), self.qs, self.qr, g, {"seq": to})
+
+    def row_all(self, g):
+        count = (ROW if g < self.relayed else SEQ) - 1
+        return self.copy(self.blocks(g, pl.ds(0, count)), self.qs, self.qr, g, {"seq": self.seq})
+
+    def side_copy(self, g):
+        head = lax.rem(self.head + 2 * (g % 2), HEADS)
         seq = (1 - self.low) * ROW + self.at
-        return remote(blocks, blocks, self.ys.at[src], self.yr.at[src], {"seq": seq, "head": head})
-
-    def core_copy(self, src, low):
-        blocks = self.half(src, low)
-        return remote(blocks, blocks, self.cs.at[src], self.cr.at[src], {"head": self.other_core})
-
-    def core_all(self, src):
-        blocks = self.buf.at[src]
-        return remote(blocks, blocks, self.cs.at[src], self.cr.at[src], {"head": self.other_core})
-
-    def first(self, i):
-        self.slot_wait(i)
-        self.row_send(i)
-
-    def second(self, i):
-        src = self.source(i)
-        self.row_all(i).wait_recv()
-        if i >= self.relayed:
-            self.core_all(src).start()
-            return
-        self.side_copy(i).start()
-        self.core_copy(src, self.low).start()
-
-    def third(self, i):
-        if i >= self.relayed:
-            return
-        src = self.source(i)
-        self.side_copy(i).wait_recv()
-        self.core_copy(src, 1 - self.low).start()
-
-    def fourth(self, i):
-        self.core_all(self.source(i, mine=False)).wait_recv()
+        near = self.blocks(g, pl.ds(self.low * ROW, ROW))
+        return self.copy(near, self.ys, self.yr, g, {"seq": seq, "head": head})
+
+    def core_copy(self, g, seqs, mine=True):
+        return self.copy(self.blocks(g, seqs, mine), self.cs, self.cr, g, {"head": self.other_core})
+
+    def first(self, g):
+        for step in range(g * STEPS_EACH, (g + 1) * STEPS_EACH):
+            self.slot_wait(step)
+        for k in range(1, ROW if g < self.relayed else SEQ):
+            self.row_copy(g, k).start()
+
+    def second(self, g):
+        self.row_all(g).wait_recv()
+        if g < self.relayed:
+            self.side_copy(g).start()
+            self.core_copy(g, pl.ds(self.low * ROW, ROW)).start()
+        else:
+            self.core_copy(g, pl.ds(0, SEQ)).start()
+
+    def third(self, g):
+        if g < self.relayed:
+            self.side_copy(g).wait_recv()
+            self.core_copy(g, pl.ds((1 - self.low) * ROW, ROW)).start()
+
+    def fourth(self, g):
+        self.core_copy(g, pl.ds(0, SEQ), False).wait_recv()
 
     def finish(self):
         @pl.when(self.own)
         def _():
-            @pl.loop(1, SLOTS)
-            def _(k):
+            for k in range(1, SLOTS):
                 self.slot_copy(k).wait_send()
 
-        for i in range(PAIRS):
-            self.row_all(i).wait_send()
-            if i < self.relayed:
-                self.side_copy(i).wait_send()
-            self.core_all(self.source(i)).wait_send()
+        for g in range(PAIRS // STEPS_EACH):
+            self.row_all(g).wait_send()
+            if g < self.relayed:
+                self.side_copy(g).wait_send()
+            self.core_copy(g, pl.ds(0, SEQ)).wait_send()
 
 
 def split(value, count):
@@ -270,8 +269,8 @@
     pr,
     *sems,
 ):
-    x = Spread(xall, 0, RELAYED, sems[:8])
-    m = Spread(mall, 1, 0, sems[8:])
+    x = Spread(xall, False, RELAYED, sems[:8])
+    m = Spread(mall, True, MOD_RELAYED, sems[8:])
     slot, seq, head = x.slot, x.seq, x.head
     loads = [
         pltpu.make_async_copy(src, dst, local_sem.at[i])
@@ -323,7 +322,7 @@
         for row in (gain, high.astype(F32), low.astype(F32)):
             rows += [row[:, 128 * r : 128 * r + 128] for r in range(PARTS)]
         rows += [jnp.zeros((1, 128), F32)]
-        mall[slot, seq] = jnp.concatenate(rows, axis=0).astype(BF16)
+        mall[0, 0, seq] = jnp.concatenate(rows, axis=0).astype(BF16)
 
     pl.semaphore_wait(barrier, SLOTS + HEADS + SEQ - 3 + 1)
     sends = [
@@ -363,7 +362,7 @@
 
     @pl.when(x.own)
     def _():
-        xall[slot, seq] = block
+        xall[0, 0, seq] = block
 
     x.slot_send()
     stepped_t[...] = jnp.transpose(stepped)
@@ -385,13 +384,11 @@
     b_q = jnp.sum(found[PATCH:own_rows], axis=0, keepdims=True)
 
     def build(k):
-        sources = [m.source(2 * k + e, mine) for e in range(2) for mine in (True, False)]
-
-        for at, src in enumerate(sources):
+        steps = [(odd, 2 * k + e) for e in range(2) for odd in (0, 1)]
+        for at, (odd, step) in enumerate(steps):
             first = at * own_rows
-
             for p in range(SEQ):
-                mods = mall[src, p].astype(F32)
+                mods = mall[1 - odd, step, p].astype(F32)
                 for r in range(PARTS):
                     lanes = slice(p * FEAT + 128 * r, p * FEAT + 128 * r + 128)
                     lhs[first : first + PATCH, lanes] = (centred[:, lanes] * mods[r : r + 1]).astype(BF16)
@@ -399,15 +396,14 @@
                     lhs[first + PATCH : first + own_rows, lanes] = kept.astype(BF16)
 
         found = jnp.dot(lhs[...], kv_weight[...], preferred_element_type=F32)
-        for at, src in enumerate(sources):
+        for at, (odd, step) in enumerate(steps):
             first = at * own_rows
-            a_kv[src] = found[first : first + PATCH].astype(BF16)
-            b_kv[src] = jnp.broadcast_to(
-                jnp.sum(found[first + PATCH : first + own_rows], axis=0, keepdims=True), (8, 2 * HD)
-            )
-
-    def tokens(src, matrix, bias):
-        blocks = xall[src].reshape(SEQ * XROWS, 128)
+            bias = jnp.sum(found[first + PATCH : first + own_rows], axis=0, keepdims=True)
+            a_kv[odd, step] = found[first : first + PATCH].astype(BF16)
+            b_kv[odd, step] = jnp.broadcast_to(bias, (8, 2 * HD))
+
+    def tokens(odd, step, matrix, bias):
+        blocks = xall[odd, step].reshape(SEQ * XROWS, 128)
         zero = jnp.zeros_like(matrix)
         found = []
         for pair in ([matrix, zero], [zero, matrix]):
@@ -420,21 +416,17 @@
     group = SEQ * HALF
     mine = slot_group[slot]
 
-    def prepare(i, own):
+    def pair(i):
         keys, values = pairs[i % 2]
-        src = x.source(i, own)
-        b = lax.rem(src + 1, SLOTS)
-        keep = jnp.full((1, HD), group_mask[mine, slot_group[b]], jnp.int32).astype(F32)
-        for half, t in enumerate(tokens(src, a_kv[b], b_kv[b][0:1])):
-            first = (half if own else 2 + half) * group
-            rows = slice(first, first + group)
-            keys[rows, :] = unit(t[:, 0:HD]).astype(BF16)
-            values[rows, 0:HD] = (t[:, HD : 2 * HD] * keep).astype(BF16)
-            values[rows, HD : 2 * HD] = jnp.broadcast_to(keep, (group, HD)).astype(BF16)
-
-    def pair(i):
-        prepare(i, True)
-        prepare(i, False)
+        for odd in (0, 1):
+            b = lax.rem(slot + offset(odd, i) + 1, SLOTS)
+            keep = jnp.full((1, HD), group_mask[mine, slot_group[b]], jnp.int32).astype(F32)
+            for half, t in enumerate(tokens(odd, i, a_kv[odd, i], b_kv[odd, i][0:1])):
+                first = (2 * odd + half) * group
+                rows = slice(first, first + group)
+                keys[rows, :] = unit(t[:, 0:HD]).astype(BF16)
+                values[rows, 0:HD] = (t[:, HD : 2 * HD] * keep).astype(BF16)
+                values[rows, HD : 2 * HD] = jnp.broadcast_to(keep, (group, HD)).astype(BF16)
 
     def attend(i):
         keys, values = pairs[i % 2]
@@ -445,7 +437,7 @@
     total[...] = jnp.zeros_like(total)
     def queries():
         scale = 1.0 / (math.sqrt(HD) * math.log(2.0))
-        for half, t in enumerate(tokens(lax.rem(slot + SLOTS - 1, SLOTS), a_q.astype(BF16), b_q)):
+        for half, t in enumerate(tokens(1, 0, a_q.astype(BF16), b_q)):
             q_ref[half * group : half * group + group, :] = (unit(t) * scale).astype(BF16)
 
     def run(what, first, last):
@@ -530,14 +522,14 @@
             vmem((D, 2 * HD), BF16),
             vmem((PATCH, TOK), F32),
             vmem((SEQ * TOK, HD), BF16),
-            vmem((SLOTS, SEQ, XROWS, 128), BF16),
-            vmem((SLOTS, SEQ, MROWS, 128), BF16),
+            vmem((2, PAIRS, SEQ, XROWS, 128), BF16),
+            vmem((2, PAIRS, SEQ, MROWS, 128), BF16),
             vmem((XROWS, 128), F32),
             vmem((HEADS - 1, XROWS, 128), F32),
             vmem((PATCH, D), F32),
             vmem((4 * (PATCH + MROWS), D), BF16),
-            vmem((SLOTS, PATCH, 2 * HD), BF16),
-            vmem((SLOTS, 8, 2 * HD), F32),
+            vmem((2, PAIRS, PATCH, 2 * HD), BF16),
+            vmem((2, PAIRS, 8, 2 * HD), F32),
             vmem((SEQ * TOK, HD), BF16),
             vmem((KEYS, HD), BF16),
             vmem((KEYS, 2 * HD), BF16),

time: 55.2 us -> 54.3 us (0.984)
  Pallas kernels: 51.4 us -> 50.5 us
    pallas_call x1, Pallas kernels: 51.4 us -> 50.5 us  [local(): pl.pallas_call(kernel, out_shape=(jax.ShapeDtypeStruct((PATCH, TOK), F32)...]
where the time goes in v6:
time: 54.3 us; the launch traced here: 54.1 us
  Pallas kernels  50.5 us (93%)
  local copies, waits for them, and re-layouts  2.97 us (5%)
  between operations  0.64 us (1%)
    pallas_call x1, Pallas kernels, local(): pl.pallas_call(kernel, out_shape=(jax.ShapeDtypeStruct((PATCH, TOK), F32)...  50.5 us
    unnamed x2, local copies, waits for them, and re-layouts  2.97 us

profile of v6, /device:TPU:1, one launch (start us, length us, event | category | flops | bytes accessed | tf_op | source)
XLA Modules:
  0.0 54.1 jit_solution(9463510512542522084)
XLA Ops:
  0.6 50.5 %window.1 = (f32[64,80]{1,0:T(8,128)}, bf16[640,128]{1,0:T(8,128)(2,1)}) custom-call(bf16[80,1280]{1,0:T(8,128)(2,1)} %hidden_in.1, f32[1,2,1280]{2,1,0:T(2,128)} %final_mod_in.1, f32[64,1280]{1,0:T(8,128)} %bitcast.6, f32[64,80]{1,0:T(8,128)} %bitcast.7, f32[64,80]{1,0:T(8,128)} %bitcast.8, s32[16]{0:T(128)} %step_in.1, s32[16]{0:T(128)} %group_in.1, ...), custom_call_target="tpu_custom_call" | custom-call | tf_op jit(solution)/shard_map/window/pallas_call | solution.py:502
  51.2 1.4 %copy.15 = f32[80,64]{0,1:T(8,128)} copy(f32[80,64]{0,1:T(8,128)} %bitcast.9) | data formatting | bytes 40960
  52.5 1.6 %copy.16 = bf16[640,128]{1,0:T(8,128)(2,1)} copy(bf16[640,128]{1,0:T(8,128)(2,1)} %get-tuple-element.9) | data formatting | bytes 327680

commit v7 on v6

--- a/solution.py
+++ b/solution.py
@@ -349,26 +349,6 @@
     later = jnp.where(slot == SLOTS - 1, 0, step_index[jnp.minimum(slot + 1, SLOTS - 1)])
     delta = sigma_of(later) - sigma_of(now)
 
-    for copy in sends:
-        copy.wait_recv()
-    velocity = whole_velocity([msg[...]] + [got[k] for k in range(HEADS - 1)], D // HEADS)
-    stepped = latents + delta * velocity
-    shifted = jnp.where(slot == SLOTS - 1, noise, stepped).astype(BF16).astype(F32)
-    projected = jnp.dot(shifted, gram, precision=HIGHEST, preferred_element_type=F32)
-    spread = jnp.sum(projected * shifted, axis=1, keepdims=True)
-    scaled = shifted * lax.rsqrt(jnp.maximum(spread, 0.0) + EPS)
-    block = jnp.concatenate([scaled[0:HALF], scaled[HALF:TOK]], axis=1)
-    block = jnp.concatenate([block, jnp.zeros((XROWS - HALF, 128), F32)], axis=0).astype(BF16)
-
-    @pl.when(x.own)
-    def _():
-        xall[0, 0, seq] = block
-
-    x.slot_send()
-    stepped_t[...] = jnp.transpose(stepped)
-    stepped_copy = pltpu.make_async_copy(stepped_t, stepped_out, local_sem.at[0])
-    stepped_copy.start()
-
     wide = weight.astype(F32)
     centred[...] = wide - jnp.mean(wide, axis=1, keepdims=True)
     own_rows = PATCH + MROWS
@@ -382,6 +362,26 @@
     found = jnp.dot(lhs[0:own_rows, :], q_weight[...], preferred_element_type=F32)
     a_q = found[0:PATCH]
     b_q = jnp.sum(found[PATCH:own_rows], axis=0, keepdims=True)
+
+    for copy in sends:
+        copy.wait_recv()
+    velocity = whole_velocity([msg[...]] + [got[k] for k in range(HEADS - 1)], D // HEADS)
+    stepped = latents + delta * velocity
+    shifted = jnp.where(slot == SLOTS - 1, noise, stepped).astype(BF16).astype(F32)
+    projected = jnp.dot(shifted, gram, precision=HIGHEST, preferred_element_type=F32)
+    spread = jnp.sum(projected * shifted, axis=1, keepdims=True)
+    scaled = shifted * lax.rsqrt(jnp.maximum(spread, 0.0) + EPS)
+    block = jnp.concatenate([scaled[0:HALF], scaled[HALF:TOK]], axis=1)
+    block = jnp.concatenate([block, jnp.zeros((XROWS - HALF, 128), F32)], axis=0).astype(BF16)
+
+    @pl.when(x.own)
+    def _():
+        xall[0, 0, seq] = block
+
+    x.slot_send()
+    stepped_t[...] = jnp.transpose(stepped)
+    stepped_copy = pltpu.make_async_copy(stepped_t, stepped_out, local_sem.at[0])
+    stepped_copy.start()
 
     def build(k):
         steps = [(odd, 2 * k + e) for e in range(2) for odd in (0, 1)]

time: 54.3 us -> 53.8 us (level)
  no operation moved by 1% of the time
where the time goes in v7:
time: 53.8 us; the launch traced here: 53.6 us
  Pallas kernels  50 us (93%)
  local copies, waits for them, and re-layouts  2.97 us (6%)
  between operations  0.64 us (1%)
    pallas_call x1, Pallas kernels, local(): pl.pallas_call(kernel, out_shape=(jax.ShapeDtypeStruct((PATCH, TOK), F32)...  50 us
    unnamed x2, local copies, waits for them, and re-layouts  2.97 us

profile of v7, /device:TPU:1, one launch (start us, length us, event | category | flops | bytes accessed | tf_op | source)
XLA Modules:
  0.0 53.6 jit_solution(6458288943149483724)
XLA Ops:
  0.6 50.0 %window.1 = (f32[64,80]{1,0:T(8,128)}, bf16[640,128]{1,0:T(8,128)(2,1)}) custom-call(bf16[80,1280]{1,0:T(8,128)(2,1)} %hidden_in.1, f32[1,2,1280]{2,1,0:T(2,128)} %final_mod_in.1, f32[64,1280]{1,0:T(8,128)} %bitcast.6, f32[64,80]{1,0:T(8,128)} %bitcast.7, f32[64,80]{1,0:T(8,128)} %bitcast.8, s32[16]{0:T(128)} %step_in.1, s32[16]{0:T(128)} %group_in.1, ...), custom_call_target="tpu_custom_call" | custom-call | tf_op jit(solution)/shard_map/window/pallas_call | solution.py:502
  50.6 1.4 %copy.15 = f32[80,64]{0,1:T(8,128)} copy(f32[80,64]{0,1:T(8,128)} %bitcast.9) | data formatting | bytes 40960
  52.0 1.6 %copy.16 = bf16[640,128]{1,0:T(8,128)(2,1)} copy(bf16[640,128]{1,0:T(8,128)(2,1)} %get-tuple-element.9) | data formatting | bytes 327680
